TPU v7x, 256 devices: a whole 4x4x8 slice. The times are simulated.
256 devices in a mesh: dp: 64 (over x, z, core), mp: 4 (over y).
Axes of the slice: x: 4, y: 4, z: 8, core: 2. Of those that a mesh axis runs over, the one named last changes fastest.
Arguments:
- features: bfloat16 [65536, 1024], P('dp'), may hold values from -6 to 6
- out_grads: bfloat16 [65536, 4, 1024], P('dp', None, 'mp'), may hold values from -0.0234375 to 0.0234375
- norm_grads: float32 [64, 2048], P('dp'), may hold values from -0.75 to 0.75
- owners: int32 [5], replicated, may hold values from 0 to 63, as said below
- moment1: float32 [4, 1024, 1024], P(None, 'dp', 'mp'), may hold values from -6 to 6
- moment2: float32 [4, 1024, 1024], P(None, 'dp', 'mp'), may hold values from 0.1 to 10
- left_stats: float32 [4, 1024, 1024], P(None, 'dp', 'mp'), may hold values from -1024 to 1024, as said below
- right_stats: float32 [4, 1024, 1024], P(None, 'dp', 'mp'), may hold values from -1024 to 1024, as said below
- left_basis: float32 [4, 1024, 1024], P(None, 'dp', 'mp'), may hold values from -1 to 2
- right_basis: float32 [4, 1024, 1024], P(None, 'dp', 'mp'), may hold values from -1 to 2
- norm_m: float32 [2048], P('dp'), may hold values from -6 to 6
- norm_v: float32 [2048], P('dp'), may hold values from 0.1 to 10
Outputs:
- new_moment1: float32 [4, 1024, 1024], P(None, 'dp', 'mp')
- new_moment2: float32 [4, 1024, 1024], P(None, 'dp', 'mp')
- new_left_stats: float32 [4, 1024, 1024], P(None, 'dp', 'mp')
- new_right_stats: float32 [4, 1024, 1024], P(None, 'dp', 'mp')
- new_left_basis: float32 [4, 1024, 1024], P(None, 'dp', 'mp')
- new_right_basis: float32 [4, 1024, 1024], P(None, 'dp', 'mp')
- update_slots: bfloat16 [64, 1024, 1024], P('dp', None, 'mp')
- new_norm_m: float32 [2048], P('dp')
- new_norm_v: float32 [2048], P('dp')
- norm_slots: float32 [64, 2048], P('dp')
Inputs may be any that keep to these rules, and one draw needn't show every extreme that they name: `owners`: the first 4 entries are distinct, so a dp index owns at most one tile; the last entry may equal any of them. `left_stats`: each tile of statistics is symmetric. `right_stats`: each tile of statistics is symmetric.
All inputs are finite; a program needn't handle non-finite values.
Results may differ from a plain program's by a relative error of at most 0.0072.
Values may be sent and summed in bfloat16 or wider, within the bound.
No kernel may reach another device: no remote copies, remote signals or barrier semaphores. Data moves between devices by JAX's collectives and lax.ppermute only.
A program may use at most 128 MiB of HBM per device.

v0:
```python
import jax
import jax.numpy as jnp
from jax import lax
from jax.experimental import pallas as pl
from jax.experimental.pallas import tpu as pltpu
from jax.sharding import Mesh, PartitionSpec as P

FIX_ONE = 1.0 - 0.9**10
FIX_TWO = 1.0 - 0.95**10
F32 = jnp.float32
BF = jnp.bfloat16
NX, NZ, NC, NM = 4, 8, 2, 4
B = 16
W = 256
PAD = 16


def contract(left, right, left_dim, right_dim):
    return lax.dot_general(
        left, right, (((left_dim,), (right_dim,)), ((), ())), preferred_element_type=F32
    )


def swap_cores(value):
    return lax.ppermute(value, "c", [(0, 1), (1, 0)])


def exchange(value, axis):
    return lax.all_to_all(value, axis, 0, 0, tiled=True)


def turn(value, s):
    return lax.ppermute(value, "mp", [(i, (i + s) % NM) for i in range(NM)])


def turn_x(value, s):
    return lax.ppermute(value, "x", [(i, (i + s) % NX) for i in range(NX)])


def all_turns(value, turn_by):
    far = turn_by(value, 2)
    return [value, turn_by(value, 1), far, turn_by(value, 3)]


def everyone(value, axis, count):
    return exchange(jnp.broadcast_to(value[None], (count, *value.shape)), axis)


def ordered(core, mine, other):
    return jnp.where(core == 0, jnp.stack([mine, other]), jnp.stack([other, mine]))


VMEM = pl.BlockSpec(memory_space=pltpu.VMEM)
SMEM = pl.BlockSpec(memory_space=pltpu.SMEM)


COST = pl.CostEstimate(flops=6 * 10**9, bytes_accessed=24 * 10**6, transcendentals=0)


def dot_nn(a, b):
    return contract(a, b, 1, 0)


def dot_nt(a, b):
    return contract(a, b, 1, 1)


def dot_tn(a, b):
    return contract(a, b, 0, 0)


def call(kernel, name, outs, scratch, *args, cost=None):
    n_scalar = 1
    return pl.pallas_call(
        kernel,
        out_shape=[jax.ShapeDtypeStruct(s, d) for s, d in outs],
        in_specs=[SMEM] * n_scalar + [VMEM] * (len(args) - n_scalar),
        out_specs=[VMEM] * len(outs),
        scratch_shapes=[pltpu.VMEM(s, d) for s, d in scratch],
        compiler_params=pltpu.CompilerParams(vmem_limit_bytes=16 * 1024 * 1024),
        cost_estimate=cost,
        name=name,
    )(*args)


def pack_kernel(*refs):
    states, outs, (held, sems) = refs[:6], refs[6:10], refs[10:]
    x, c = lax.axis_index("x"), lax.axis_index("c")
    copies = [pltpu.make_async_copy(ref, held.at[k], sems.at[k]) for k, ref in enumerate(states)]
    for copy in copies:
        copy.start()
    for copy in copies:
        copy.wait()
    for shift, out in enumerate(outs):
        tile = lax.rem(x + shift, NX)
        for k in range(4):
            out[k] = held[k, tile].astype(BF)
        lefts, rights = held[4, tile], held[5, tile]
        out[4] = jnp.where(c == 0, lefts, rights).astype(BF)
        out[5] = jnp.where(c == 0, rights, lefts).astype(BF)


def join_kernel(*refs):
    *parts, out = refs
    start = 0
    for part in parts:
        out[start : start + part.shape[0]] = part[...]
        start += part.shape[0]


def join(*parts):
    shape = (sum(p.shape[0] for p in parts), *parts[0].shape[1:])
    return pl.pallas_call(
        join_kernel,
        out_shape=jax.ShapeDtypeStruct(shape, parts[0].dtype),
        in_specs=[VMEM] * len(parts),
        out_specs=VMEM,
        name="join",
    )(*parts)


def sum_kernel(a0, a1, a2, a3, out):
    size = out.shape[1] - PAD
    half = size * NZ

    def added(rows):
        total = a0[rows].astype(F32)
        for ref in (a1, a2, a3):
            total += ref[rows].astype(F32)
        return total.astype(BF)

    norm = added(slice(half, half + PAD))
    for z in range(NZ):
        out[z, :size] = added(slice(z * size, (z + 1) * size))
        out[z, size:] = norm


def spread_kernel(r0, r1, r2, r3, trigger, bases, moments, keep, send):
    for s, ref in enumerate((r0, r1, r2, r3)):
        for k in range(2):
            bases[NX * k + s] = ref[k]
            moments[NX * k + s] = ref[2 + k]
        keep[s] = ref[4]
        send[s] = ref[5]


def choose_kernel(keep, other, trigger, stats, near, far):
    x, m = lax.axis_index("x"), lax.axis_index("mp")
    stats[:NX] = keep[...]
    stats[NX:] = other[...]
    for out, steps in ((near, (0, 1)), (far, (0, 2))):
        for j, step in enumerate(steps):
            shift = lax.rem(x - lax.rem(m + step, NM) + NX, NX)
            out[j] = keep[shift]
            out[2 + j] = other[shift]


def small(kernel, name, counts, *args):
    return pl.pallas_call(
        kernel,
        out_shape=[jax.ShapeDtypeStruct((n, B, W), BF) for n in counts],
        in_specs=[VMEM] * (len(args) - 1) + [pl.BlockSpec(memory_space=pl.ANY)],
        out_specs=[VMEM] * len(counts),
        name=name,
    )(*args)


def block_start(index, size):
    return pl.multiple_of(index * size, size)


def shift_of(where, xp):
    return lax.rem(where[0] - xp + NX, NX)


def prep_kernel(where, own, oth, left, right):
    c, m = where[2], where[3]
    for shift in range(NX):
        start = shift_of(where, shift) * (NZ * NC * B)
        for t in range(NM):
            col = block_start(lax.rem(m - t + NM, NM), W)
            for z in range(NZ):
                for ref, core in ((own, c), (oth, 1 - c)):
                    row = pl.multiple_of(start + z * (NC * B) + core * B, B)
                    left[pl.ds(row, B), pl.ds(col, W)] = ref[z, 2 * NX * t + shift]
                    right[pl.ds(row, B), pl.ds(col, W)] = ref[z, 2 * NX * t + NX + shift]


def old_power_kernel(where, pack, left, right, out, block):
    c, m = where[2], where[3]

    def fill(n, piece):
        for z in range(NZ):
            for k, core in ((0, c), (1, 1 - c)):
                row = pl.multiple_of(z * (NC * B) + core * B, B)
                block[n, pl.ds(row, B), :] = piece(z, k)

    for u in range(NM):
        shift = shift_of(where, lax.rem(m + u, NM))
        fill(u, lambda z, k: pack[z, NX * k + shift])
    for n in range(3):
        for j in range(2):
            fill(4 + 2 * n + j, lambda z, k: pack[z, 8 + 4 * n + 2 * k + j])
    table = (
        ((0, 0), (1, 1), (2, 1), (3, 1)),
        ((1, 0), (6, 0), (7, 1), (5, 0)),
        ((2, 0), (7, 0), (8, 0), (9, 1)),
        ((3, 0), (5, 1), (9, 0), (4, 0)),
    )

    def product(basis):
        for u in range(NM):
            total = None
            for v in range(NM):
                rows = basis[pl.ds(block_start(lax.rem(m + v, NM), W), W), :]
                place, turned = table[u][v]
                part = (dot_tn if turned else dot_nn)(block[place], rows)
                total = part if total is None else total + part
            out[pl.ds(block_start(lax.rem(m + u, NM), W), W), :] = total

    @pl.when(c == 0)
    def _():
        product(left)

    @pl.when(c == 1)
    def _():
        product(right)


def rotate_kernel(where, *refs):
    own, oth = refs[:NM], refs[NM : 2 * NM]
    left, right, pack, grad, work, direct, rot_home, rot = refs[2 * NM :]
    z, c, m = where[1], where[2], where[3]
    half = own[0].shape[0]
    for pieces, core in ((own, c), (oth, 1 - c)):
        r = pl.ds(block_start(core, half), half)
        for s in range(NM):
            grad[r, pl.ds(block_start(lax.rem(m - s + NM, NM), W), W)] = pieces[s][...]
    col = pl.ds(block_start(m, W), W)

    @pl.when(c == 0)
    def _():
        work[...] = dot_tn(left[...], grad[...]).astype(BF)
        rot[...] = dot_nn(work[...], right[:, col])

    @pl.when(c == 1)
    def _():
        work[...] = dot_nn(grad[...], right[...]).astype(BF)
        rot[...] = dot_tn(left[...], work[:, col])

    for xp in range(NX):
        shift = shift_of(where, xp)
        for zp in range(NZ):
            k = xp * NZ + zp
            value = rot[pl.ds(pl.multiple_of(k * (NC * B) + c * B, B), B), :]
            one = 0.9 * pack[zp, 8 * NX + shift].astype(F32) + 0.1 * value
            two = 0.95 * pack[zp, 9 * NX + shift].astype(F32) + 0.05 * value * value
            value = (one / FIX_ONE / (jnp.sqrt(two / FIX_TWO) + 1e-08)).astype(BF)
            for copy in range(NM):
                direct[copy, k * B : (k + 1) * B, :] = value
    for xp in range(NX):
        row = pl.multiple_of(xp * (NZ * NC * B) + z * (NC * B) + c * B, B)
        rot_home[xp] = rot[pl.ds(row, B), :].astype(BF)


def power_kernel(where, grad, work, old, outer, basis, power, iterate):
    z, c, m = where[1], where[2], where[3]
    col = pl.ds(block_start(m, W), W)
    total = NM * W

    def z_rows(xp):
        return pl.ds(pl.multiple_of(xp * (NZ * NC * B) + z * (NC * B), NC * B), NC * B)

    @pl.when(c == 0)
    def _():
        def rows(i, sums):
            r = pl.ds(block_start(i, W), W)
            value = 0.95 * old[r, :] + 0.05 * dot_nt(grad[r, :], work[...])
            power[r, :] = value
            return sums + jnp.sum(value * value, axis=0, keepdims=True)

        sums = lax.fori_loop(0, NM, rows, jnp.zeros((1, total), F32))
        scale = lax.rsqrt(sums + 1e-06)
        for i in range(NM):
            r = slice(i * W, (i + 1) * W)
            iterate[r, :] = (power[r, :] * scale).astype(BF)
        for xp in range(NX):
            outer[xp] = dot_nt(grad[z_rows(xp), :], grad[col, :]).astype(BF)

    @pl.when(c == 1)
    def _():
        def rows(i, sums):
            r = pl.ds(block_start(i, W), W)
            value = 0.95 * old[r, :] + 0.05 * dot_tn(grad[:, r], work[...])
            power[r, :] = value
            return sums + jnp.sum(value * value, axis=0, keepdims=True)

        sums = lax.fori_loop(0, NM, rows, jnp.zeros((1, total), F32))
        scale = lax.rsqrt(sums + 1e-06)
        for i in range(NM):
            r = slice(i * W, (i + 1) * W)
            iterate[r, :] = (power[r, :] * scale).astype(BF)

        def gram_rows(i, carry):
            r = pl.ds(block_start(i, W), W)
            power[r, 0:W] = dot_tn(grad[:, r], grad[:, col])
            return carry

        lax.fori_loop(0, NM, gram_rows, 0)
        for xp in range(NX):
            outer[xp] = power[z_rows(xp), 0:W].astype(BF)

    gram = dot_tn(iterate[:, col], iterate[...]).astype(BF)
    for xp in range(NX):
        here = iterate[z_rows(xp), :]
        value = 1.5 * iterate[z_rows(xp), col].astype(F32) - 0.5 * dot_nt(here, gram)
        basis[xp] = value.astype(BF)


def back_kernel(where, direct, right, back):
    m = where[3]
    rows = pl.ds(block_start(m, W), W)
    total = dot_nt(direct[0], right[rows, 0:W])
    for k in range(1, NM):
        total += dot_nt(direct[k], right[rows, k * W : (k + 1) * W])
    back[...] = total.astype(BF)


def update_kernel(
    where, own, oth, left, rot_home, outer, basis, norm, s0, s1, s2, s3, back
):
    c = where[2]
    half = own.shape[0]

    def step(k, carry):
        src = pl.ds(block_start(k, B), B)
        for ref, core in ((own, c), (oth, 1 - c)):
            back[pl.ds(pl.multiple_of(k * (NC * B) + core * B, B), B), :] = ref[src, :]
        return carry

    lax.fori_loop(0, NX * NZ, step, 0)
    value = dot_nn(left[pl.ds(block_start(c, half), half), :], back[...]).astype(BF)
    for s, out in enumerate((s0, s1, s2, s3)):
        xp = lax.rem(where[0] + s, NX)
        out[:half] = value
        out[half : half + B] = rot_home[xp]
        out[half + B : half + 3 * B] = outer[xp]
        out[half + 3 * B : half + 5 * B] = basis[xp]
        out[half + 5 * B :] = norm[...]


def relay_kernel(where, g0, g1, g2, g3, own_slot, sent):
    c = where[2]
    half = own_slot.shape[0]
    nb = NX * B
    for out, hit, tile in ((own_slot, where[4], where[5]), (sent, where[6], where[7])):
        place = shift_of(where, tile)

        @pl.when(hit == 0)
        def _():
            out[:half] = jnp.zeros((half, W), BF)

        for s, ref in enumerate((g0, g1, g2, g3)):

            @pl.when((hit > 0) & (place == s))
            def _():
                out[:half] = ref[:half]

    row = pl.multiple_of((1 - c) * B, B)
    for s, ref in enumerate((g0, g1, g2, g3)):
        outer = ref[pl.ds(half + B + row, B)]
        basis = ref[pl.ds(half + 3 * B + row, B)]
        sent[half + s * B : half + (s + 1) * B] = outer
        sent[half + nb + s * B : half + nb + (s + 1) * B] = basis
        sent[half + 2 * nb + s * PAD : half + 2 * nb + (s + 1) * PAD] = ref[half + 5 * B :]


def final_kernel(
    where,
    g0,
    g1,
    g2,
    g3,
    own_slot,
    recv,
    m1,
    m2,
    sl,
    sr,
    o1,
    o2,
    osl,
    osr,
    obl,
    obr,
    slot,
    norm,
):
    c = where[2]
    half = own_slot.shape[0]
    nb = NX * B
    slot[0, pl.ds(block_start(c, half), half)] = own_slot[...]
    slot[0, pl.ds(block_start(1 - c, half), half)] = recv[:half]
    row = pl.multiple_of(c * B, B)
    for s, ref in enumerate((g0, g1, g2, g3)):
        t = shift_of(where, s)
        other = recv[half + 2 * nb + s * PAD : half + 2 * nb + (s + 1) * PAD].astype(F32)
        value = (ref[half + 5 * B :].astype(F32) + other)[0:2]
        norm[t] = jnp.where(where[8] > 0, value, 0.0)
        rot = ref[half : half + B].astype(F32)
        o1[t] = 0.9 * m1[t] + 0.1 * rot
        o2[t] = 0.95 * m2[t] + 0.05 * rot * rot
        outer_own = ref[pl.ds(half + B + row, B)].astype(F32)
        outer_oth = recv[half + s * B : half + (s + 1) * B].astype(F32)
        basis_own = ref[pl.ds(half + 3 * B + row, B)].astype(F32)
        basis_oth = recv[half + nb + s * B : half + nb + (s + 1) * B].astype(F32)
        osl[t] = 0.95 * sl[t] + 0.05 * jnp.where(c == 0, outer_own, outer_oth)
        osr[t] = 0.95 * sr[t] + 0.05 * jnp.where(c == 0, outer_oth, outer_own)
        obl[t] = jnp.where(c == 0, basis_own, basis_oth)
        obr[t] = jnp.where(c == 0, basis_oth, basis_own)


def shards(
    features,
    out_grads,
    norm_grads,
    owners,
    moment1,
    moment2,
    left_stats,
    right_stats,
    left_basis,
    right_basis,
    norm_m,
    norm_v,
):
    xi = lax.axis_index("x")
    zi = lax.axis_index("z")
    ci = lax.axis_index("c")
    mi = lax.axis_index("mp")
    mine_dp = (xi * NZ + zi) * NC + ci
    other_dp = (xi * NZ + zi) * NC + (1 - ci)
    left_core = ci == 0
    half = features.shape[1] // 2
    full = 2 * half
    tile_owner = owners[:NX]

    def owned(index):
        hit = tile_owner == index
        which = jnp.sum(jnp.where(hit, jnp.arange(NX, dtype=jnp.int32), 0))
        return [jnp.any(hit).astype(jnp.int32), which]

    where = jnp.stack([xi, zi, ci, mi, *owned(mine_dp), *owned(other_dp), mine_dp == owners[NX]])
    where = where.astype(jnp.int32)

    with jax.named_scope("state_rows"):
        home = pl.pallas_call(
            pack_kernel,
            out_shape=[jax.ShapeDtypeStruct((6, B, W), BF)] * NX,
            in_specs=[pl.BlockSpec(memory_space=pl.ANY)] * 6,
            out_specs=[VMEM] * NX,
            scratch_shapes=[pltpu.VMEM((6, NX, B, W), F32), pltpu.SemaphoreType.DMA((6,))],
            name="pack",
        )(left_basis, right_basis, moment1, moment2, left_stats, right_stats)
        rows = [home[0]] + [
            lax.ppermute(home[s], "x", [(i, (i + s) % NX) for i in range(NX)]) for s in (1, 2, 3)
        ]
    with jax.named_scope("grad_sum"):
        feat_other = lax.dynamic_slice_in_dim(features, (1 - ci) * half, half, 1)
        feat_mine = lax.dynamic_slice_in_dim(features, ci * half, half, 1)
        norm = jnp.pad(norm_grads.reshape(NX, 2, W), ((0, 0), (0, PAD - 2), (0, 0)))

        def partial(feat):
            return jnp.einsum("ti,tnc->nic", feat, out_grads, preferred_element_type=F32)

        sent = jnp.concatenate([partial(feat_other).astype(BF), norm.astype(BF)], axis=1)
        *rows, sent = lax.optimization_barrier((*rows, sent))
        got = swap_cores(sent)
        acc = jnp.concatenate([partial(feat_mine), norm], axis=1) + got.astype(F32)
        acc = acc.astype(BF)
        bases, moments, keep, send = small(spread_kernel, "spread", (8, 8, 4, 4), *rows, acc)
        turned = [turn(bases, s) for s in (1, 2, 3)]
        pack = join(bases, *turned, moments)
        pack = lax.all_gather(pack, "z", axis=0)
        tile = lambda s: lax.dynamic_index_in_dim(acc, lax.rem(xi + s, NX), 0, keepdims=False)
        acc = [tile(0)] + [
            lax.ppermute(tile(s), "x", [(i, (i + s) % NX) for i in range(NX)]) for s in (2, 1, 3)
        ]

    with jax.named_scope("grad_sum"):
        acc = pl.pallas_call(
            sum_kernel,
            out_shape=jax.ShapeDtypeStruct((NZ, half // NZ + PAD, W), BF),
            in_specs=[VMEM] * NX,
            out_specs=VMEM,
            cost_estimate=pl.CostEstimate(
                flops=10**6, bytes_accessed=300000000, transcendentals=0
            ),
            name="sum_x",
        )(*acc)
        stats, near, far = small(choose_kernel, "choose", (8, 4, 4), keep, swap_cores(send), acc)
        stats = join(stats, turn(far, 1), turn(near, 3), turn(near, 2))
        acc = exchange(acc, "z")
        acc, stats = lax.optimization_barrier((acc, stats))
        stats = lax.all_gather(stats, "z", axis=0)
        acc = jnp.sum(acc.astype(F32), axis=0)
        grad_rows = acc[: half // NZ].astype(BF)
        norm_total = lax.dynamic_slice(
            acc[half // NZ : half // NZ + 2].reshape(-1), ((zi * NC + ci) * 32,), (32,)
        )

    new_nm = 0.9 * norm_m + 0.1 * norm_total
    new_nv = 0.95 * norm_v + 0.05 * norm_total * norm_total
    norm_step = new_nm / FIX_ONE / (jnp.sqrt(new_nv / FIX_TWO) + 1e-08)

    with jax.named_scope("grad_all"):
        norm_row = jnp.pad(norm_step.astype(BF)[None], ((0, PAD - 1), (0, W - 32)))
        grad_z = everyone(jnp.concatenate([grad_rows, norm_row], axis=0), "z", NZ)
        norm_zs = grad_z[:, half // NZ, None, :32]
        norm_zs = jnp.where(jnp.arange(NC)[None, :, None] == ci, norm_zs, 0).reshape(2, W)
        grad_half = grad_z[:, : half // NZ].reshape(half, W)
        grad_own = all_turns(grad_half, turn)
        pack, norm_zs = lax.optimization_barrier((pack, norm_zs))
        pack_other = swap_cores(pack)
        left, right = call(
            prep_kernel,
            "prep",
            [((full, full), BF)] * 2,
            [],
            where,
            pack,
            pack_other,
        )
        grad_own[2], left, right = lax.optimization_barrier((grad_own[2], left, right))
        grad_other = [swap_cores(piece) for piece in grad_own]

    with jax.named_scope("rotate"):
        grad, work, direction, rot_home = call(
            rotate_kernel,
            "rotate",
            [
                ((full, full), BF),
                ((full, full), BF),
                ((NM, half, W), BF),
                ((NX, B, W), BF),
            ],
            [((full, W), F32)],
            where,
            *grad_own,
            *grad_other,
            left,
            right,
            pack,
        )
        stats, rot_home = lax.optimization_barrier((stats, rot_home))
        direction = exchange(direction, "mp")
    with jax.named_scope("power"):
        (power_old,) = call(
            old_power_kernel,
            "old_power",
            [((full, full), F32)],
            [((10, W, W), BF)],
            where,
            stats,
            left,
            right,
            cost=COST,
        )
        outer, basis = call(
            power_kernel,
            "power",
            [((NX, NC * B, W), BF)] * 2,
            [((full, full), F32), ((full, full), BF)],
            where,
            grad,
            work,
            power_old,
            cost=COST,
        )
        norm_pad = jnp.pad(norm_zs, ((0, PAD - 2), (0, 0)))
        direction, outer, basis = lax.optimization_barrier((direction, outer, basis))
    with jax.named_scope("update"):
        (back,) = call(back_kernel, "back", [((half, W), BF)], [], where, direction, right)
        back_other = swap_cores(back)
        update = call(
            update_kernel,
            "update",
            [((half + 5 * B + PAD, W), BF)] * NX,
            [((full, W), BF)],
            where,
            back,
            back_other,
            left,
            rot_home,
            outer,
            basis,
            norm_pad,
        )

    with jax.named_scope("home"):
        update = [update[0]] + [turn_x(update[s], s) for s in (1, 2, 3)]
        nb = NX * B
        own_slot, sent = call(
            relay_kernel,
            "relay",
            [((half, W), BF), ((half + 2 * nb + NX * PAD, W), BF)],
            [],
            where,
            *update,
        )
        recv = swap_cores(sent)
        state = ((NX, B, W), F32)
        outs = call(
            final_kernel,
            "final",
            [state] * 6 + [((1, full, W), BF), ((NX, 2, W), F32)],
            [],
            where,
            *update,
            own_slot,
            recv,
            moment1,
            moment2,
            left_stats,
            right_stats,
        )
    *outs, norm_slot = outs
    return (*outs, new_nm, new_nv, norm_slot.reshape(1, -1))


def solution(mesh):
    mesh = Mesh(mesh.devices.reshape(NX, NZ, NC, NM), ("x", "z", "c", "mp"))
    dp = ("x", "z", "c")
    state = P(None, dp, "mp")
    in_specs = (
        P(dp, None),
        P(dp, None, "mp"),
        P(dp, None),
        P(),
        state,
        state,
        state,
        state,
        state,
        state,
        P(dp),
        P(dp),
    )
    out_specs = (
        state,
        state,
        state,
        state,
        state,
        state,
        P(dp, None, "mp"),
        P(dp),
        P(dp),
        P(dp, None),
    )
    return jax.shard_map(shards, mesh=mesh, in_specs=in_specs, out_specs=out_specs, check_vma=False)
```

profile of v0, /device:TPU:1, one launch (start us, length us, event | category | flops | bytes accessed | tf_op | source)
XLA Modules:
  0.0 186.6 jit_solution(10582333903427547153)
XLA Ops:
  7.2 1.9 %pack.1 = (bf16[6,16,256]{2,1,0:T(8,128)(2,1)}, bf16[6,16,256]{2,1,0:T(8,128)(2,1)}, bf16[6,16,256]{2,1,0:T(8,128)(2,1)}, bf16[6,16,256]{2,1,0:T(8,128)(2,1)}) custom-call(f32[4,16,256]{2,1,0:T(8,128)} %refs_0_.1, f32[4,16,256]{2,1,0:T(8,128)} %refs_1_.1, f32[4,16,256]{2,1,0:T(8,128)} %m1.1, f32[4,16,256]{2,1,0:T(8,128)} %m2.1, f32[4,16,256]{2,1,0:T(8,128)} %sl.1, ...), custom_call_target="tpu_custom_call" | custom-call | tf_op jit(solution)/shard_map/state_rows/pack/pallas_call | solution.py:457
  9.1 2.1 %collective-permute-start = (bf16[6,16,256]{2,1,0:T(8,128)(2,1)}, bf16[6,16,256]{2,1,0:T(8,128)(2,1)S(1)}, u32[]{:S(2)}, u32[]{:S(2)}) collective-permute-start(bf16[6,16,256]{2,1,0:T(8,128)(2,1)} %get-tuple-element.61), channel_id=1, source_target_pairs={{0,64},{64,128},{128,192},{192,0},{1,65},{65,129},{129,193},{193,1... | collective-permute-start | bytes 147464 | tf_op jit(solution)/shard_map/state_rows/ppermute | solution.py:466
  11.2 2.5 %collective-permute-start.1 = (bf16[6,16,256]{2,1,0:T(8,128)(2,1)}, bf16[6,16,256]{2,1,0:T(8,128)(2,1)S(1)}, u32[]{:S(2)}, u32[]{:S(2)}) collective-permute-start(bf16[6,16,256]{2,1,0:T(8,128)(2,1)} %get-tuple-element.62), channel_id=1, source_target_pairs={{0,128},{64,192},{128,0},{192,64},{1,129},{65,193},{129,1},{193,65... | collective-permute-start | bytes 147464 | tf_op jit(solution)/shard_map/state_rows/ppermute | solution.py:466
  13.7 1.2 collective-permute-start.2
  15.4 1.4 reduce.3
  16.8 2.5 %fusion.11 = bf16[4,512,256]{2,1,0:T(8,128)(2,1)S(1)} fusion(bf16[1024,4,256]{2,1,0:T(4,128)(2,1)S(1)} %copy-done, bf16[1024,1024]{1,0:T(8,128)(2,1)} %param.12, s32[]{:T(128)S(6)} %select_n.40), kind=kOutput, calls=%fused_computation.8 | convolution fusion | flops 1074266112 | bytes 4194308 | tf_op jit(solution)/shard_map/grad_sum/ti,tnc->nic/dot_general | solution.py:474
  19.4 1.6 collective-permute-start.3
  21.0 2.5 %fusion.5 = f32[4,512,256]{2,1,0:T(8,128)S(1)} fusion(bf16[1024,4,256]{2,1,0:T(4,128)(2,1)S(1)} %copy-done, bf16[1024,1024]{1,0:T(8,128)(2,1)} %param.12, s32[]{:T(128)S(6)} %select_n.39), kind=kOutput, calls=%fused_computation.6 | convolution fusion | flops 1073741824 | bytes 5242884 | tf_op jit(solution)/shard_map/grad_sum/ti,tnc->nic/dot_general | solution.py:474
  23.6 2.6 %fusion.trigger = bf16[4,528,256]{2,1,0:T(8,128)(2,1)} fusion(f32[4,16,256]{2,1,0:T(8,128)S(1)} %pad.12, f32[4,512,256]{2,1,0:T(8,128)S(1)} %fusion.5, bf16[4,528,256]{2,1,0:T(8,128)(2,1)} %collective-permute-done.3), kind=kLoop, calls=%fused_computation.1 | loop fusion | flops 2162688 | bytes 4325376 | tf_op jit(solution)/shard_map/grad_sum/convert_element_type | solution.py:480
  26.2 1.6 spread.1
  27.8 1.3 collective-permute-start.13
  29.1 2.6 %collective-permute-start.14 = (bf16[8,16,256]{2,1,0:T(8,128)(2,1)}, bf16[8,16,256]{2,1,0:T(8,128)(2,1)S(1)}, u32[]{:S(2)}, u32[]{:S(2)}) collective-permute-start(bf16[8,16,256]{2,1,0:T(8,128)(2,1)} %get-tuple-element.75.refs_0_), channel_id=1, source_target_pairs={{0,2},{1,3},{2,0},{3,1},{4,6},{5,7},{6,4},{7,5},{8,10},{9,11},{10,... | collective-permute-start | bytes 196616 | tf_op jit(solution)/shard_map/grad_sum/ppermute | solution.py:33
  31.7 1.1 collective-permute-start.15
  32.8 2.2 %collective-permute-done.14.refs_2_ = bf16[8,16,256]{2,1,0:T(8,128)(2,1)S(1)} collective-permute-done((bf16[8,16,256]{2,1,0:T(8,128)(2,1)}, bf16[8,16,256]{2,1,0:T(8,128)(2,1)S(1)}, u32[]{:S(2)}, u32[]{:S(2)}) %collective-permute-start.14) | collective-permute-done | bytes 65568 | tf_op jit(solution)/shard_map/grad_sum/ppermute | solution.py:33
  36.0 1.7 join.3
  37.8 0.8 dynamic-slice_bitcast_fusion
  38.5 0.9 collective-permute-start.4
  39.7 2.4 %collective-permute-start.6 = (bf16[528,256]{1,0:T(8,128)(2,1)S(1)}, bf16[528,256]{1,0:T(8,128)(2,1)S(1)}, u32[]{:S(2)}, u32[]{:S(2)}) collective-permute-start(bf16[528,256]{1,0:T(8,128)(2,1)S(1)} %get-tuple-element.117), channel_id=1, source_target_pairs={{0,192},{64,0},{128,64},{192,128},{1,193},{65,1},{129,65},{193,129... | collective-permute-start | bytes 811016 | tf_op jit(solution)/shard_map/grad_sum/ppermute | solution.py:487
  42.1 4.2 %collective-permute-done.4.a1 = bf16[528,256]{1,0:T(8,128)(2,1)S(1)} collective-permute-done((bf16[528,256]{1,0:T(8,128)(2,1)S(1)}, bf16[528,256]{1,0:T(8,128)(2,1)S(1)}, u32[]{:S(2)}, u32[]{:S(2)}) %collective-permute-start.4) | collective-permute-done | bytes 270368 | tf_op jit(solution)/shard_map/grad_sum/ppermute | solution.py:487
  46.3 7.9 %collective-permute-done.5.a2 = bf16[528,256]{1,0:T(8,128)(2,1)S(1)} collective-permute-done((bf16[528,256]{1,0:T(8,128)(2,1)S(1)}, bf16[528,256]{1,0:T(8,128)(2,1)S(1)}, u32[]{:S(2)}, u32[]{:S(2)}) %collective-permute-start.5) | collective-permute-done | bytes 270368 | tf_op jit(solution)/shard_map/grad_sum/ppermute | solution.py:487
  54.2 0.7 copy-done.21
  55.0 2.1 %sum_x.1.trigger = bf16[8,80,256]{2,1,0:T(8,128)(2,1)} custom-call(bf16[528,256]{1,0:T(8,128)(2,1)} %get-tuple-element.120.a0, bf16[528,256]{1,0:T(8,128)(2,1)} %copy-done.20, bf16[528,256]{1,0:T(8,128)(2,1)} %copy-done.21, bf16[528,256]{1,0:T(8,128)(2,1)} %copy-done.22), custom_call_target="tpu_custom_call" | custom-call | flops 1000000 | bytes 300000000 | tf_op jit(solution)/shard_map/grad_sum/sum_x/pallas_call | solution.py:491
  57.1 8.3 %all-to-all-start = ((bf16[8,80,256]{2,1,0:T(8,128)(2,1)}), bf16[8,80,256]{2,1,0:T(8,128)(2,1)S(1)}, u32[]{:S(2)}, u32[]{:S(2)}) async-start(bf16[8,80,256]{2,1,0:T(8,128)(2,1)} %sum_x.1.trigger), calls=%async_computation | async-start | bytes 655360 | tf_op jit(solution)/shard_map/grad_sum/all_to_all | solution.py:29
  65.4 0.8 collective-permute-start.7
  66.2 0.9 collective-permute-done.7.other
  67.7 1.4 choose.1
  69.1 2.7 %collective-permute-start.9 = (bf16[4,16,256]{2,1,0:T(8,128)(2,1)}, bf16[4,16,256]{2,1,0:T(8,128)(2,1)S(1)}, u32[]{:S(2)}, u32[]{:S(2)}) collective-permute-start(bf16[4,16,256]{2,1,0:T(8,128)(2,1)} %get-tuple-element.73), channel_id=1, source_target_pairs={{0,3},{1,0},{2,1},{3,2},{4,7},{5,4},{6,5},{7,6},{8,11},{9,8},{10,9... | collective-permute-start | bytes 98312 | tf_op jit(solution)/shard_map/grad_sum/ppermute | solution.py:33
  72.5 1.2 collective-permute-done.8.refs_1_
  73.7 2.9 %collective-permute-done.10.refs_3_ = bf16[4,16,256]{2,1,0:T(8,128)(2,1)S(1)} collective-permute-done((bf16[4,16,256]{2,1,0:T(8,128)(2,1)}, bf16[4,16,256]{2,1,0:T(8,128)(2,1)S(1)}, u32[]{:S(2)}, u32[]{:S(2)}) %collective-permute-start.10) | collective-permute-done | bytes 32800 | tf_op jit(solution)/shard_map/grad_sum/ppermute | solution.py:33
  77.2 1.5 join.2
  78.7 2.9 %all-to-all-done = bf16[8,80,256]{2,1,0:T(8,128)(2,1)S(1)} async-done(((bf16[8,80,256]{2,1,0:T(8,128)(2,1)}), bf16[8,80,256]{2,1,0:T(8,128)(2,1)S(1)}, u32[]{:S(2)}, u32[]{:S(2)}) %all-to-all-start) | async-done | bytes 327712 | tf_op jit(solution)/shard_map/grad_sum/all_to_all | solution.py:29
  82.4 0.7 broadcast_in_dim.39
  83.1 3.8 %all-to-all-start.1 = ((bf16[8,80,256]{2,1,0:T(8,128)(2,1)}), bf16[8,80,256]{2,1,0:T(8,128)(2,1)S(1)}, u32[]{:S(2)}, u32[]{:S(2)}) async-start(bf16[8,80,256]{2,1,0:T(8,128)(2,1)} %broadcast_in_dim.39), calls=%async_computation.1 | async-start | bytes 655360 | tf_op jit(solution)/shard_map/grad_all/all_to_all | solution.py:29
  86.9 10.4 %all-to-all-done.1 = bf16[8,80,256]{2,1,0:T(8,128)(2,1)S(1)} async-done(((bf16[8,80,256]{2,1,0:T(8,128)(2,1)}), bf16[8,80,256]{2,1,0:T(8,128)(2,1)S(1)}, u32[]{:S(2)}, u32[]{:S(2)}) %all-to-all-start.1) | async-done | bytes 327712 | tf_op jit(solution)/shard_map/grad_all/all_to_all | solution.py:29
  97.5 3.9 %collective-permute-start.16 = (bf16[8,40,16,256]{3,2,1,0:T(8,128)(2,1)}, bf16[8,40,16,256]{3,2,1,0:T(8,128)(2,1)}, u32[]{:S(2)}, u32[]{:S(2)}) collective-permute-start(bf16[8,40,16,256]{3,2,1,0:T(8,128)(2,1)} %bitcast.41), channel_id=1, source_target_pairs={{0,4},{4,0},{1,5},{5,1},{2,6},{6,2},{3,7},{7,3},{8,12},{12,8},{9,1... | collective-permute-start | bytes 7864328 | tf_op jit(solution)/shard_map/grad_all/ppermute | solution.py:25
  101.6 2.5 %collective-permute-start.17 = (bf16[512,256]{1,0:T(8,128)(2,1)S(1)}, bf16[512,256]{1,0:T(8,128)(2,1)S(1)}, u32[]{:S(2)}, u32[]{:S(2)}) collective-permute-start(bf16[512,256]{1,0:T(8,128)(2,1)S(1)} %bitcast.45), channel_id=1, source_target_pairs={{0,3},{1,0},{2,1},{3,2},{4,7},{5,4},{6,5},{7,6},{8,11},{9,8},{10,9... | collective-permute-start | bytes 786440 | tf_op jit(solution)/shard_map/grad_all/ppermute | solution.py:33
  108.5 1.4 stack.51.where
  110.7 0.7 collective-permute-start.19
  111.4 3.6 %collective-permute-done.17.refs_3_ = bf16[512,256]{1,0:T(8,128)(2,1)S(1)} collective-permute-done((bf16[512,256]{1,0:T(8,128)(2,1)S(1)}, bf16[512,256]{1,0:T(8,128)(2,1)S(1)}, u32[]{:S(2)}, u32[]{:S(2)}) %collective-permute-start.17) | collective-permute-done | bytes 262176 | tf_op jit(solution)/shard_map/grad_all/ppermute | solution.py:33
  115.0 1.3 collective-permute-start.21
  116.3 1.8 copy-done.1
  118.1 2.6 %prep.1 = (bf16[1024,1024]{1,0:T(8,128)(2,1)S(1)}, bf16[1024,1024]{1,0:T(8,128)(2,1)S(1)}) custom-call(s32[9]{0:T(128)S(1)} %stack.51.where, bf16[8,40,16,256]{3,2,1,0:T(8,128)(2,1)S(1)} %bitcast.42, bf16[8,40,16,256]{3,2,1,0:T(8,128)(2,1)} %collective-permute-done.16.oth), custom_call_target="tpu_custom_call" | custom-call | tf_op jit(solution)/shard_map/grad_all/prep/pallas_call | solution.py:74
  120.9 1.5 collective-permute-done.20.refs_6_
  122.4 5.5 %rotate.1 = (bf16[1024,1024]{1,0:T(8,128)(2,1)S(1)}, bf16[1024,1024]{1,0:T(8,128)(2,1)S(1)}, bf16[4,512,256]{2,1,0:T(8,128)(2,1)S(1)}, bf16[4,16,256]{2,1,0:T(8,128)(2,1)S(1)}) custom-call(s32[9]{0:T(128)S(1)} %stack.51.where, bf16[512,256]{1,0:T(8,128)(2,1)S(1)} %bitcast.48, bf16[512,256]{1,0:T(8,128)(2,1)S(1)} %collective-permute-done.11.refs_1_, ...), custom_call_target="tpu_custom_call" | custom-call | tf_op jit(solution)/shard_map/rotate/rotate/pallas_call | solution.py:74
  127.9 0.9 copy-done.9
  128.9 1.3 copy-done.14
  130.2 1.4 copy-done.16
  131.6 4.6 %all-to-all-start.2 = ((bf16[4,512,256]{2,1,0:T(8,128)(2,1)}), bf16[4,512,256]{2,1,0:T(8,128)(2,1)S(1)}, u32[]{:S(2)}, u32[]{:S(2)}) async-start(bf16[4,512,256]{2,1,0:T(8,128)(2,1)} %copy-done.9), calls=%async_computation.2 | async-start | bytes 2097152 | tf_op jit(solution)/shard_map/rotate/all_to_all | solution.py:29
  136.3 1.6 copy-done.4
  137.8 1.6 copy-done.7
  139.4 1.3 copy-done.18
  140.8 3.0 %old_power.1.old = f32[1024,1024]{1,0:T(8,128)S(1)} custom-call(s32[9]{0:T(128)S(1)} %stack.51.where, bf16[8,20,16,256]{3,2,1,0:T(8,128)(2,1)S(1)} %bitcast.49, bf16[1024,1024]{1,0:T(8,128)(2,1)S(1)} %copy-done.4, bf16[1024,1024]{1,0:T(8,128)(2,1)S(1)} %copy-done.7), custom_call_target="tpu_custom_call" | custom-call | flops 6000000000 | bytes 24000000 | tf_op jit(solution)/shard_map/power/old_power/pallas_call | solution.py:74
  143.8 6.9 %power.1 = (bf16[4,32,256]{2,1,0:T(8,128)(2,1)S(1)}, bf16[4,32,256]{2,1,0:T(8,128)(2,1)S(1)}) custom-call(s32[9]{0:T(128)S(1)} %stack.51.where, bf16[1024,1024]{1,0:T(8,128)(2,1)S(1)} %copy-done.15, bf16[1024,1024]{1,0:T(8,128)(2,1)S(1)} %copy-done.17, f32[1024,1024]{1,0:T(8,128)S(1)} %old_power.1.old), custom_call_target="tpu_custom_call" | custom-call | flops 6000000000 | bytes 24000000 | tf_op jit(solution)/shard_map/power/power/pallas_call | solution.py:74
  150.7 0.8 all-to-all-done.2.direct
  151.5 1.7 copy-done.8
  153.2 1.0 back.1.own
  154.8 1.2 collective-permute-done.22.oth
  155.9 1.2 update.1
  157.7 1.2 collective-permute-start.24
  158.9 1.3 collective-permute-start.25
  160.2 13.5 %collective-permute-done.23.g1 = bf16[608,256]{1,0:T(8,128)(2,1)S(1)} collective-permute-done((bf16[608,256]{1,0:T(8,128)(2,1)S(1)}, bf16[608,256]{1,0:T(8,128)(2,1)S(1)}, u32[]{:S(2)}, u32[]{:S(2)}) %collective-permute-start.23) | collective-permute-done | bytes 311328 | tf_op jit(solution)/shard_map/home/ppermute | solution.py:37
  174.7 1.6 collective-permute-start.26
  176.3 1.3 collective-permute-done.26.recv
  177.6 1.5 final.1
  (119 shorter events, 11.1 us)
Async XLA Ops:
  7.2 9.6 %copy-start = (bf16[1024,4,256]{2,1,0:T(4,128)(2,1)S(1)}, bf16[1024,4,256]{2,1,0:T(4,128)(2,1)}, u32[]{:S(2)}) copy-start(bf16[1024,4,256]{2,1,0:T(4,128)(2,1)} %param.13) | copy-start | bytes 6291460
  7.2 90.3 %all-gather.5.cloned.1.call-start = ((), (), s32[]{:S(2)}) async-start(), calls=%async_computation.3 | async-start | bytes 2949120 | tf_op jit(solution)/shard_map/grad_sum/all_gather | solution.py:484
  9.1 10.2 %collective-permute-start = (bf16[6,16,256]{2,1,0:T(8,128)(2,1)}, bf16[6,16,256]{2,1,0:T(8,128)(2,1)S(1)}, u32[]{:S(2)}, u32[]{:S(2)}) collective-permute-start(bf16[6,16,256]{2,1,0:T(8,128)(2,1)} %get-tuple-element.61), channel_id=1, source_target_pairs={{0,64},{64,128},{128,192},{192,0},{1,65},{65,129},{129,193},{193,1... | collective-permute-start | bytes 147464 | tf_op jit(solution)/shard_map/state_rows/ppermute | solution.py:466
  11.2 8.1 %collective-permute-start.1 = (bf16[6,16,256]{2,1,0:T(8,128)(2,1)}, bf16[6,16,256]{2,1,0:T(8,128)(2,1)S(1)}, u32[]{:S(2)}, u32[]{:S(2)}) collective-permute-start(bf16[6,16,256]{2,1,0:T(8,128)(2,1)} %get-tuple-element.62), channel_id=1, source_target_pairs={{0,128},{64,192},{128,0},{192,64},{1,129},{65,193},{129,1},{193,65... | collective-permute-start | bytes 147464 | tf_op jit(solution)/shard_map/state_rows/ppermute | solution.py:466
  13.7 5.7 %collective-permute-start.2 = (bf16[6,16,256]{2,1,0:T(8,128)(2,1)}, bf16[6,16,256]{2,1,0:T(8,128)(2,1)S(1)}, u32[]{:S(2)}, u32[]{:S(2)}) collective-permute-start(bf16[6,16,256]{2,1,0:T(8,128)(2,1)} %get-tuple-element.63), channel_id=1, source_target_pairs={{0,192},{64,0},{128,64},{192,128},{1,193},{65,1},{129,65},{193,129... | collective-permute-start | bytes 147464 | tf_op jit(solution)/shard_map/state_rows/ppermute | solution.py:466
  19.4 4.2 %copy-start.26 = (bf16[6,16,256]{2,1,0:T(8,128)(2,1)}, bf16[6,16,256]{2,1,0:T(8,128)(2,1)S(1)}, u32[]{:S(2)}) copy-start(bf16[6,16,256]{2,1,0:T(8,128)(2,1)S(1)} %collective-permute-done.r1) | copy-start | bytes 147460
  19.4 4.2 %copy-start.27 = (bf16[6,16,256]{2,1,0:T(8,128)(2,1)}, bf16[6,16,256]{2,1,0:T(8,128)(2,1)S(1)}, u32[]{:S(2)}) copy-start(bf16[6,16,256]{2,1,0:T(8,128)(2,1)S(1)} %collective-permute-done.1.r2) | copy-start | bytes 147460
  19.4 4.1 %copy-start.28 = (bf16[6,16,256]{2,1,0:T(8,128)(2,1)}, bf16[6,16,256]{2,1,0:T(8,128)(2,1)S(1)}, u32[]{:S(2)}) copy-start(bf16[6,16,256]{2,1,0:T(8,128)(2,1)S(1)} %collective-permute-done.2.r3) | copy-start | bytes 147460
  19.4 4.1 %collective-permute-start.3 = (bf16[4,528,256]{2,1,0:T(8,128)(2,1)S(1)}, bf16[4,528,256]{2,1,0:T(8,128)(2,1)}, u32[]{:S(2)}, u32[]{:S(2)}) collective-permute-start(bf16[4,528,256]{2,1,0:T(8,128)(2,1)S(1)} %pad_maximum_fusion), channel_id=1, source_target_pairs={{0,4},{4,0},{1,5},{5,1},{2,6},{6,2},{3,7},{7,3},{8,12},{12,8},{9,1... | collective-permute-start | bytes 3244040 | tf_op jit(solution)/shard_map/grad_sum/ppermute | solution.py:25
  26.1 11.6 %copy-start.19 = (bf16[4,528,256]{2,1,0:T(8,128)(2,1)S(1)}, bf16[4,528,256]{2,1,0:T(8,128)(2,1)}, u32[]{:S(2)}) copy-start(bf16[4,528,256]{2,1,0:T(8,128)(2,1)} %fusion.trigger) | copy-start | bytes 3244036
  27.8 5.0 %collective-permute-start.13 = (bf16[8,16,256]{2,1,0:T(8,128)(2,1)}, bf16[8,16,256]{2,1,0:T(8,128)(2,1)S(1)}, u32[]{:S(2)}, u32[]{:S(2)}) collective-permute-start(bf16[8,16,256]{2,1,0:T(8,128)(2,1)} %get-tuple-element.75.refs_0_), channel_id=1, source_target_pairs={{0,1},{1,2},{2,3},{3,0},{4,5},{5,6},{6,7},{7,4},{8,9},{9,10},{10,1... | collective-permute-start | bytes 196616 | tf_op jit(solution)/shard_map/grad_sum/ppermute | solution.py:33
  29.1 5.9 %collective-permute-start.14 = (bf16[8,16,256]{2,1,0:T(8,128)(2,1)}, bf16[8,16,256]{2,1,0:T(8,128)(2,1)S(1)}, u32[]{:S(2)}, u32[]{:S(2)}) collective-permute-start(bf16[8,16,256]{2,1,0:T(8,128)(2,1)} %get-tuple-element.75.refs_0_), channel_id=1, source_target_pairs={{0,2},{1,3},{2,0},{3,1},{4,6},{5,7},{6,4},{7,5},{8,10},{9,11},{10,... | collective-permute-start | bytes 196616 | tf_op jit(solution)/shard_map/grad_sum/ppermute | solution.py:33
  31.7 3.6 %collective-permute-start.15 = (bf16[8,16,256]{2,1,0:T(8,128)(2,1)}, bf16[8,16,256]{2,1,0:T(8,128)(2,1)S(1)}, u32[]{:S(2)}, u32[]{:S(2)}) collective-permute-start(bf16[8,16,256]{2,1,0:T(8,128)(2,1)} %get-tuple-element.75.refs_0_), channel_id=1, source_target_pairs={{0,3},{1,0},{2,1},{3,2},{4,7},{5,4},{6,5},{7,6},{8,11},{9,8},{10,9... | collective-permute-start | bytes 196616 | tf_op jit(solution)/shard_map/grad_sum/ppermute | solution.py:33
  32.8 2.6 %copy-start.23 = (bf16[8,16,256]{2,1,0:T(8,128)(2,1)}, bf16[8,16,256]{2,1,0:T(8,128)(2,1)S(1)}, u32[]{:S(2)}) copy-start(bf16[8,16,256]{2,1,0:T(8,128)(2,1)S(1)} %collective-permute-done.13.refs_1_) | copy-start | bytes 196612
  37.7 27.6 %copy-start.36 = (bf16[4,16,256]{2,1,0:T(8,128)(2,1)S(1)}, bf16[4,16,256]{2,1,0:T(8,128)(2,1)}, u32[]{:S(2)}) copy-start(bf16[4,16,256]{2,1,0:T(8,128)(2,1)} %get-tuple-element.70) | copy-start | bytes 98308
  38.5 43.2 %copy-start.34 = (f32[32]{0:T(128)S(1)}, f32[32]{0:T(128)}, u32[]{:S(2)}) copy-start(f32[32]{0:T(128)} %param.22) | copy-start | bytes 388
  38.5 43.2 %copy-start.35 = (f32[32]{0:T(128)S(1)}, f32[32]{0:T(128)}, u32[]{:S(2)}) copy-start(f32[32]{0:T(128)} %param.23) | copy-start | bytes 388
  38.5 7.8 %collective-permute-start.4 = (bf16[528,256]{1,0:T(8,128)(2,1)S(1)}, bf16[528,256]{1,0:T(8,128)(2,1)S(1)}, u32[]{:S(2)}, u32[]{:S(2)}) collective-permute-start(bf16[528,256]{1,0:T(8,128)(2,1)S(1)} %get-tuple-element.119), channel_id=1, source_target_pairs={{0,128},{64,192},{128,0},{192,64},{1,129},{65,193},{129,1},{193,65... | collective-permute-start | bytes 811016 | tf_op jit(solution)/shard_map/grad_sum/ppermute | solution.py:487
  39.4 14.8 %collective-permute-start.5 = (bf16[528,256]{1,0:T(8,128)(2,1)S(1)}, bf16[528,256]{1,0:T(8,128)(2,1)S(1)}, u32[]{:S(2)}, u32[]{:S(2)}) collective-permute-start(bf16[528,256]{1,0:T(8,128)(2,1)S(1)} %get-tuple-element.118), channel_id=1, source_target_pairs={{0,64},{64,128},{128,192},{192,0},{1,65},{65,129},{129,193},{193,1... | collective-permute-start | bytes 811016 | tf_op jit(solution)/shard_map/grad_sum/ppermute | solution.py:487
  39.7 14.6 %collective-permute-start.6 = (bf16[528,256]{1,0:T(8,128)(2,1)S(1)}, bf16[528,256]{1,0:T(8,128)(2,1)S(1)}, u32[]{:S(2)}, u32[]{:S(2)}) collective-permute-start(bf16[528,256]{1,0:T(8,128)(2,1)S(1)} %get-tuple-element.117), channel_id=1, source_target_pairs={{0,192},{64,0},{128,64},{192,128},{1,193},{65,1},{129,65},{193,129... | collective-permute-start | bytes 811016 | tf_op jit(solution)/shard_map/grad_sum/ppermute | solution.py:487
  46.3 7.9 %copy-start.20 = (bf16[528,256]{1,0:T(8,128)(2,1)}, bf16[528,256]{1,0:T(8,128)(2,1)S(1)}, u32[]{:S(2)}) copy-start(bf16[528,256]{1,0:T(8,128)(2,1)S(1)} %collective-permute-done.4.a1) | copy-start | bytes 811012
  54.2 0.8 copy-start.22
  57.1 47.5 %copy-start.33 = (s32[5]{0:T(128)S(1)}, s32[5]{0:T(128)}, u32[]{:S(2)}) copy-start(s32[5]{0:T(128)} %param.15) | copy-start | bytes 64
  57.1 24.5 %all-to-all-start = ((bf16[8,80,256]{2,1,0:T(8,128)(2,1)}), bf16[8,80,256]{2,1,0:T(8,128)(2,1)S(1)}, u32[]{:S(2)}, u32[]{:S(2)}) async-start(bf16[8,80,256]{2,1,0:T(8,128)(2,1)} %sum_x.1.trigger), calls=%async_computation | async-start | bytes 655360 | tf_op jit(solution)/shard_map/grad_sum/all_to_all | solution.py:29
  65.4 1.7 collective-permute-start.7
  69.1 4.6 %collective-permute-start.8 = (bf16[4,16,256]{2,1,0:T(8,128)(2,1)}, bf16[4,16,256]{2,1,0:T(8,128)(2,1)S(1)}, u32[]{:S(2)}, u32[]{:S(2)}) collective-permute-start(bf16[4,16,256]{2,1,0:T(8,128)(2,1)} %get-tuple-element.72), channel_id=1, source_target_pairs={{0,1},{1,2},{2,3},{3,0},{4,5},{5,6},{6,7},{7,4},{8,9},{9,10},{10,1... | collective-permute-start | bytes 98312 | tf_op jit(solution)/shard_map/grad_sum/ppermute | solution.py:33
  69.1 4.6 %collective-permute-start.9 = (bf16[4,16,256]{2,1,0:T(8,128)(2,1)}, bf16[4,16,256]{2,1,0:T(8,128)(2,1)S(1)}, u32[]{:S(2)}, u32[]{:S(2)}) collective-permute-start(bf16[4,16,256]{2,1,0:T(8,128)(2,1)} %get-tuple-element.73), channel_id=1, source_target_pairs={{0,3},{1,0},{2,1},{3,2},{4,7},{5,4},{6,5},{7,6},{8,11},{9,8},{10,9... | collective-permute-start | bytes 98312 | tf_op jit(solution)/shard_map/grad_sum/ppermute | solution.py:33
  71.8 4.8 %collective-permute-start.10 = (bf16[4,16,256]{2,1,0:T(8,128)(2,1)}, bf16[4,16,256]{2,1,0:T(8,128)(2,1)S(1)}, u32[]{:S(2)}, u32[]{:S(2)}) collective-permute-start(bf16[4,16,256]{2,1,0:T(8,128)(2,1)} %get-tuple-element.73), channel_id=1, source_target_pairs={{0,2},{1,3},{2,0},{3,1},{4,6},{5,7},{6,4},{7,5},{8,10},{9,11},{10,... | collective-permute-start | bytes 98312 | tf_op jit(solution)/shard_map/grad_sum/ppermute | solution.py:33
  73.7 2.9 %copy-start.29 = (bf16[4,16,256]{2,1,0:T(8,128)(2,1)}, bf16[4,16,256]{2,1,0:T(8,128)(2,1)S(1)}, u32[]{:S(2)}) copy-start(bf16[4,16,256]{2,1,0:T(8,128)(2,1)S(1)} %collective-permute-done.8.refs_1_) | copy-start | bytes 98308
  73.7 2.9 %copy-start.30 = (bf16[4,16,256]{2,1,0:T(8,128)(2,1)}, bf16[4,16,256]{2,1,0:T(8,128)(2,1)S(1)}, u32[]{:S(2)}) copy-start(bf16[4,16,256]{2,1,0:T(8,128)(2,1)S(1)} %collective-permute-done.9.refs_2_) | copy-start | bytes 98308
  83.1 14.2 %all-to-all-start.1 = ((bf16[8,80,256]{2,1,0:T(8,128)(2,1)}), bf16[8,80,256]{2,1,0:T(8,128)(2,1)S(1)}, u32[]{:S(2)}, u32[]{:S(2)}) async-start(bf16[8,80,256]{2,1,0:T(8,128)(2,1)} %broadcast_in_dim.39), calls=%async_computation.1 | async-start | bytes 655360 | tf_op jit(solution)/shard_map/grad_all/all_to_all | solution.py:29
  86.9 49.4 %all-gather.7.cloned.1.call-start = ((), (), s32[]{:S(2)}) async-start(), calls=%async_computation.4 | async-start | bytes 1474560 | tf_op jit(solution)/shard_map/grad_sum/all_gather | solution.py:505
  97.5 18.8 %collective-permute-start.16 = (bf16[8,40,16,256]{3,2,1,0:T(8,128)(2,1)}, bf16[8,40,16,256]{3,2,1,0:T(8,128)(2,1)}, u32[]{:S(2)}, u32[]{:S(2)}) collective-permute-start(bf16[8,40,16,256]{3,2,1,0:T(8,128)(2,1)} %bitcast.41), channel_id=1, source_target_pairs={{0,4},{4,0},{1,5},{5,1},{2,6},{6,2},{3,7},{7,3},{8,12},{12,8},{9,1... | collective-permute-start | bytes 7864328 | tf_op jit(solution)/shard_map/grad_all/ppermute | solution.py:25
  101.4 9.3 %collective-permute-start.11 = (bf16[512,256]{1,0:T(8,128)(2,1)S(1)}, bf16[512,256]{1,0:T(8,128)(2,1)S(1)}, u32[]{:S(2)}, u32[]{:S(2)}) collective-permute-start(bf16[512,256]{1,0:T(8,128)(2,1)S(1)} %bitcast.44), channel_id=1, source_target_pairs={{0,1},{1,2},{2,3},{3,0},{4,5},{5,6},{6,7},{7,4},{8,9},{9,10},{10,1... | collective-permute-start | bytes 786440 | tf_op jit(solution)/shard_map/grad_all/ppermute | solution.py:33
  101.6 13.4 %collective-permute-start.17 = (bf16[512,256]{1,0:T(8,128)(2,1)S(1)}, bf16[512,256]{1,0:T(8,128)(2,1)S(1)}, u32[]{:S(2)}, u32[]{:S(2)}) collective-permute-start(bf16[512,256]{1,0:T(8,128)(2,1)S(1)} %bitcast.45), channel_id=1, source_target_pairs={{0,3},{1,0},{2,1},{3,2},{4,7},{5,4},{6,5},{7,6},{8,11},{9,8},{10,9... | collective-permute-start | bytes 786440 | tf_op jit(solution)/shard_map/grad_all/ppermute | solution.py:33
  104.2 16.6 %collective-permute-start.12 = (bf16[512,256]{1,0:T(8,128)(2,1)S(1)}, bf16[512,256]{1,0:T(8,128)(2,1)S(1)}, u32[]{:S(2)}, u32[]{:S(2)}) collective-permute-start(bf16[512,256]{1,0:T(8,128)(2,1)S(1)} %bitcast.46), channel_id=1, source_target_pairs={{0,2},{1,3},{2,0},{3,1},{4,6},{5,7},{6,4},{7,5},{8,10},{9,11},{10,... | collective-permute-start | bytes 786440 | tf_op jit(solution)/shard_map/grad_all/ppermute | solution.py:33
  109.8 11.0 %collective-permute-start.18 = (bf16[512,256]{1,0:T(8,128)(2,1)S(1)}, bf16[512,256]{1,0:T(8,128)(2,1)S(1)}, u32[]{:S(2)}, u32[]{:S(2)}) collective-permute-start(bf16[512,256]{1,0:T(8,128)(2,1)S(1)} %bitcast.47), channel_id=1, source_target_pairs={{0,4},{4,0},{1,5},{5,1},{2,6},{6,2},{3,7},{7,3},{8,12},{12,8},{9,1... | collective-permute-start | bytes 786440 | tf_op jit(solution)/shard_map/grad_all/ppermute | solution.py:25
  110.7 10.1 %collective-permute-start.19 = (bf16[512,256]{1,0:T(8,128)(2,1)S(1)}, bf16[512,256]{1,0:T(8,128)(2,1)S(1)}, u32[]{:S(2)}, u32[]{:S(2)}) collective-permute-start(bf16[512,256]{1,0:T(8,128)(2,1)S(1)} %collective-permute-done.11.refs_1_), channel_id=1, source_target_pairs={{0,4},{4,0},{1,5},{5,1},{2,6},{6,2},{3,7},{7,3},{8,12},{12,8},{9,1... | collective-permute-start | bytes 786440 | tf_op jit(solution)/shard_map/grad_all/ppermute | solution.py:25
  115.0 5.8 %collective-permute-start.21 = (bf16[512,256]{1,0:T(8,128)(2,1)S(1)}, bf16[512,256]{1,0:T(8,128)(2,1)S(1)}, u32[]{:S(2)}, u32[]{:S(2)}) collective-permute-start(bf16[512,256]{1,0:T(8,128)(2,1)S(1)} %collective-permute-done.17.refs_3_), channel_id=1, source_target_pairs={{0,4},{4,0},{1,5},{5,1},{2,6},{6,2},{3,7},{7,3},{8,12},{12,8},{9,1... | collective-permute-start | bytes 786440 | tf_op jit(solution)/shard_map/grad_all/ppermute | solution.py:25
  116.3 1.8 copy-start.1
  118.1 4.3 %copy-start.2 = (bf16[320,16,256]{2,1,0:T(8,128)(2,1)S(1)}, bf16[320,16,256]{2,1,0:T(8,128)(2,1)}, u32[]{:S(2)}) copy-start(bf16[320,16,256]{2,1,0:T(8,128)(2,1)} %all-gather.5.cloned.1.call-done) | copy-start | bytes 7864324
  120.7 7.2 %copy-start.3 = (bf16[1024,1024]{1,0:T(8,128)(2,1)}, bf16[1024,1024]{1,0:T(8,128)(2,1)S(1)}, u32[]{:S(2)}) copy-start(bf16[1024,1024]{1,0:T(8,128)(2,1)S(1)} %get-tuple-element.81.refs_8_.left) | copy-start | bytes 6291460
  120.7 7.2 %copy-start.6 = (bf16[1024,1024]{1,0:T(8,128)(2,1)}, bf16[1024,1024]{1,0:T(8,128)(2,1)S(1)}, u32[]{:S(2)}) copy-start(bf16[1024,1024]{1,0:T(8,128)(2,1)S(1)} %get-tuple-element.82.refs_9_.right) | copy-start | bytes 6291460
  120.7 1.6 collective-permute-start.20
  127.9 1.0 copy-start.9
  128.9 1.3 copy-start.14
  130.2 1.4 copy-start.16
  131.6 19.9 %all-to-all-start.2 = ((bf16[4,512,256]{2,1,0:T(8,128)(2,1)}), bf16[4,512,256]{2,1,0:T(8,128)(2,1)S(1)}, u32[]{:S(2)}, u32[]{:S(2)}) async-start(bf16[4,512,256]{2,1,0:T(8,128)(2,1)} %copy-done.9), calls=%async_computation.2 | async-start | bytes 2097152 | tf_op jit(solution)/shard_map/rotate/all_to_all | solution.py:29
  136.3 1.6 copy-start.4
  137.8 1.6 copy-start.7
  139.4 1.3 copy-start.18
  140.8 3.0 %copy-start.15 = (bf16[1024,1024]{1,0:T(8,128)(2,1)S(1)}, bf16[1024,1024]{1,0:T(8,128)(2,1)}, u32[]{:S(2)}) copy-start(bf16[1024,1024]{1,0:T(8,128)(2,1)} %copy-done.14) | copy-start | bytes 6291460
  140.8 3.0 %copy-start.17 = (bf16[1024,1024]{1,0:T(8,128)(2,1)S(1)}, bf16[1024,1024]{1,0:T(8,128)(2,1)}, u32[]{:S(2)}) copy-start(bf16[1024,1024]{1,0:T(8,128)(2,1)} %copy-done.16) | copy-start | bytes 6291460
  151.5 4.5 %copy-start.5 = (bf16[1024,1024]{1,0:T(8,128)(2,1)S(1)}, bf16[1024,1024]{1,0:T(8,128)(2,1)}, u32[]{:S(2)}) copy-start(bf16[1024,1024]{1,0:T(8,128)(2,1)} %copy-done.3) | copy-start | bytes 6291460
  151.5 1.7 copy-start.8
  154.2 23.3 %copy-start.10 = (f32[4,16,256]{2,1,0:T(8,128)S(1)}, f32[4,16,256]{2,1,0:T(8,128)}, u32[]{:S(2)}) copy-start(f32[4,16,256]{2,1,0:T(8,128)} %m1.1) | copy-start | bytes 196612
  154.2 23.3 %copy-start.11 = (f32[4,16,256]{2,1,0:T(8,128)S(1)}, f32[4,16,256]{2,1,0:T(8,128)}, u32[]{:S(2)}) copy-start(f32[4,16,256]{2,1,0:T(8,128)} %m2.1) | copy-start | bytes 196612
  154.3 23.3 %copy-start.12 = (f32[4,16,256]{2,1,0:T(8,128)S(1)}, f32[4,16,256]{2,1,0:T(8,128)}, u32[]{:S(2)}) copy-start(f32[4,16,256]{2,1,0:T(8,128)} %sl.1) | copy-start | bytes 196612
  154.3 23.3 %copy-start.13 = (f32[4,16,256]{2,1,0:T(8,128)S(1)}, f32[4,16,256]{2,1,0:T(8,128)}, u32[]{:S(2)}) copy-start(f32[4,16,256]{2,1,0:T(8,128)} %sr.1) | copy-start | bytes 196612
  154.3 1.6 collective-permute-start.22
  157.2 16.5 %collective-permute-start.23 = (bf16[608,256]{1,0:T(8,128)(2,1)S(1)}, bf16[608,256]{1,0:T(8,128)(2,1)S(1)}, u32[]{:S(2)}, u32[]{:S(2)}) collective-permute-start(bf16[608,256]{1,0:T(8,128)(2,1)S(1)} %get-tuple-element.97), channel_id=1, source_target_pairs={{0,64},{64,128},{128,192},{192,0},{1,65},{65,129},{129,193},{193,1... | collective-permute-start | bytes 933896 | tf_op jit(solution)/shard_map/home/ppermute | solution.py:37
  157.7 16.0 %collective-permute-start.24 = (bf16[608,256]{1,0:T(8,128)(2,1)S(1)}, bf16[608,256]{1,0:T(8,128)(2,1)S(1)}, u32[]{:S(2)}, u32[]{:S(2)}) collective-permute-start(bf16[608,256]{1,0:T(8,128)(2,1)S(1)} %get-tuple-element.98), channel_id=1, source_target_pairs={{0,128},{64,192},{128,0},{192,64},{1,129},{65,193},{129,1},{193,65... | collective-permute-start | bytes 933896 | tf_op jit(solution)/shard_map/home/ppermute | solution.py:37
  158.9 15.1 %collective-permute-start.25 = (bf16[608,256]{1,0:T(8,128)(2,1)S(1)}, bf16[608,256]{1,0:T(8,128)(2,1)S(1)}, u32[]{:S(2)}, u32[]{:S(2)}) collective-permute-start(bf16[608,256]{1,0:T(8,128)(2,1)S(1)} %get-tuple-element.99), channel_id=1, source_target_pairs={{0,192},{64,0},{128,64},{192,128},{1,193},{65,1},{129,65},{193,129... | collective-permute-start | bytes 933896 | tf_op jit(solution)/shard_map/home/ppermute | solution.py:37
  174.7 2.9 %collective-permute-start.26 = (bf16[704,256]{1,0:T(8,128)(2,1)S(1)}, bf16[704,256]{1,0:T(8,128)(2,1)S(1)}, u32[]{:S(2)}, u32[]{:S(2)}) collective-permute-start(bf16[704,256]{1,0:T(8,128)(2,1)S(1)} %get-tuple-element.101), channel_id=1, source_target_pairs={{0,4},{4,0},{1,5},{5,1},{2,6},{6,2},{3,7},{7,3},{8,12},{12,8},{9,1... | collective-permute-start | bytes 1081352 | tf_op jit(solution)/shard_map/home/ppermute | solution.py:25
  (5 other events, 3.2 us)
Sparse Core Ops, SparseCore 0:
  37.8 48.2 all-gather.4
  101.5 28.2 all-gather.6
where the time goes:
time: 188 us; the launch traced here: 187 us
  waiting for transfers between devices  55.5 us (30%)
  starting transfers between devices  51.7 us (28%)
  Pallas kernels  32.8 us (17%)
  local copies, waits for them, and re-layouts  19.2 us (10%)
  between operations  16.5 us (9%)
  other arithmetic  6.03 us (3%)
  matrix products  4.99 us (3%)
    pallas_call x8, Pallas kernels, call(): pl.pallas_call(kernel, out_shape=[jax.ShapeDtypeStruct(s, d) for s, d in...  22.5 us
    all_to_all x3, starting transfers between devices, exchange(): return lax.all_to_all(value, axis, 0, 0, tiled=True)  16.7 us
    unnamed x78, local copies, waits for them, and re-layouts  14.9 us
    all_to_all x3, waiting for transfers between devices, exchange(): return lax.all_to_all(value, axis, 0, 0, tiled=True)  14 us
    ppermute x3, waiting for transfers between devices, turn_x(): return lax.ppermute(value, 'x', [(i, (i + s) % NX) for i in range(NX)])  13.9 us
    ppermute x3, waiting for transfers between devices, shards(): lax.ppermute(tile(s), 'x', [(i, (i + s) % NX) for i in range(NX)])  12.1 us
    ppermute x9, starting transfers between devices, turn(): return lax.ppermute(value, 'mp', [(i, (i + s) % NM) for i in range(NM)])  11.6 us
    ppermute x9, starting transfers between devices, swap_cores(): return lax.ppermute(value, 'c', [(0, 1), (1, 0)])  11 us
  transfers between devices with their start and end apart: 32, of which 17 were waited for; matrix products, arithmetic and copies ran while one was open for 7% of the time, Pallas kernels for 12%

commit v1 on v0

--- a/solution.py
+++ b/solution.py
@@ -117,6 +117,12 @@
         out_specs=VMEM,
         name="join",
     )(*parts)
+
+
+def norm_kernel(row, out):
+    out[...] = jnp.zeros(out.shape, F32)
+    for k in range(2 * NX):
+        out[k // 2, k % 2 : k % 2 + 1] = row[:, k * W : (k + 1) * W]
 
 
 def sum_kernel(a0, a1, a2, a3, out):
@@ -468,7 +474,13 @@
     with jax.named_scope("grad_sum"):
         feat_other = lax.dynamic_slice_in_dim(features, (1 - ci) * half, half, 1)
         feat_mine = lax.dynamic_slice_in_dim(features, ci * half, half, 1)
-        norm = jnp.pad(norm_grads.reshape(NX, 2, W), ((0, 0), (0, PAD - 2), (0, 0)))
+        norm = pl.pallas_call(
+            norm_kernel,
+            out_shape=jax.ShapeDtypeStruct((NX, PAD, W), F32),
+            in_specs=[VMEM],
+            out_specs=VMEM,
+            name="norm_rows",
+        )(norm_grads)
 
         def partial(feat):
             return jnp.einsum("ti,tnc->nic", feat, out_grads, preferred_element_type=F32)
@@ -499,6 +511,7 @@
             name="sum_x",
         )(*acc)
         stats, near, far = small(choose_kernel, "choose", (8, 4, 4), keep, swap_cores(send), acc)
+        acc, where = lax.optimization_barrier((acc, where))
         stats = join(stats, turn(far, 1), turn(near, 3), turn(near, 2))
         acc = exchange(acc, "z")
         acc, stats = lax.optimization_barrier((acc, stats))

time: 188 us -> 188 us (level)
    ppermute x9, waiting for transfers between devices: 10.6 us -> 15.7 us  [turn(): return lax.ppermute(value, 'mp', [(i, (i + s) % NM) for i in range(NM)])]
    ppermute x3, waiting for transfers between devices: 12.1 us -> 7.21 us  [shards(): lax.ppermute(tile(s), 'x', [(i, (i + s) % NX) for i in range(NX)])]
    unnamed x78 -> x79, local copies, waits for them, and re-layouts: 14.9 us -> 14.4 us
  transfers between devices with their start and end apart: 32 -> 32, of which waited for: 17 -> 15; matrix products, arithmetic and copies ran while one was open for 7% -> 6% of each run, Pallas kernels for 12% -> 13%
where the time goes in v1:
time: 188 us; the launch traced here: 187 us
  waiting for transfers between devices  56.8 us (30%)
  starting transfers between devices  50.5 us (27%)
  Pallas kernels  34.1 us (18%)
  local copies, waits for them, and re-layouts  18.8 us (10%)
  between operations  16.5 us (9%)
  other arithmetic  5.49 us (3%)
  matrix products  5.01 us (3%)
    pallas_call x8, Pallas kernels, call(): pl.pallas_call(kernel, out_shape=[jax.ShapeDtypeStruct(s, d) for s, d in...  22.5 us
    all_to_all x3, starting transfers between devices, exchange(): return lax.all_to_all(value, axis, 0, 0, tiled=True)  16.1 us
    ppermute x9, waiting for transfers between devices, turn(): return lax.ppermute(value, 'mp', [(i, (i + s) % NM) for i in range(NM)])  15.7 us
    all_to_all x3, waiting for transfers between devices, exchange(): return lax.all_to_all(value, axis, 0, 0, tiled=True)  15.2 us
    unnamed x79, local copies, waits for them, and re-layouts  14.4 us
    ppermute x3, waiting for transfers between devices, turn_x(): return lax.ppermute(value, 'x', [(i, (i + s) % NX) for i in range(NX)])  13.9 us
    ppermute x9, starting transfers between devices, turn(): return lax.ppermute(value, 'mp', [(i, (i + s) % NM) for i in range(NM)])  11.3 us
    ppermute x9, starting transfers between devices, swap_cores(): return lax.ppermute(value, 'c', [(0, 1), (1, 0)])  10.8 us
  transfers between devices with their start and end apart: 32, of which 15 were waited for; matrix products, arithmetic and copies ran while one was open for 6% of the time, Pallas kernels for 13%

profile of v1, /device:TPU:1, one launch (start us, length us, event | category | flops | bytes accessed | tf_op | source)
XLA Modules:
  0.0 187.2 jit_solution(13720168791881433124)
XLA Ops:
  7.2 1.9 %pack.1 = (bf16[6,16,256]{2,1,0:T(8,128)(2,1)}, bf16[6,16,256]{2,1,0:T(8,128)(2,1)}, bf16[6,16,256]{2,1,0:T(8,128)(2,1)}, bf16[6,16,256]{2,1,0:T(8,128)(2,1)}) custom-call(f32[4,16,256]{2,1,0:T(8,128)} %refs_0_.1, f32[4,16,256]{2,1,0:T(8,128)} %refs_1_.1, f32[4,16,256]{2,1,0:T(8,128)} %m1.1, f32[4,16,256]{2,1,0:T(8,128)} %m2.1, f32[4,16,256]{2,1,0:T(8,128)} %sl.1, ...), custom_call_target="tpu_custom_call" | custom-call | tf_op jit(solution)/shard_map/state_rows/pack/pallas_call | solution.py:463
  9.1 2.1 %collective-permute-start = (bf16[6,16,256]{2,1,0:T(8,128)(2,1)}, bf16[6,16,256]{2,1,0:T(8,128)(2,1)S(1)}, u32[]{:S(2)}, u32[]{:S(2)}) collective-permute-start(bf16[6,16,256]{2,1,0:T(8,128)(2,1)} %get-tuple-element.63), channel_id=1, source_target_pairs={{0,64},{64,128},{128,192},{192,0},{1,65},{65,129},{129,193},{193,1... | collective-permute-start | bytes 147464 | tf_op jit(solution)/shard_map/state_rows/ppermute | solution.py:472
  11.2 2.5 %collective-permute-start.1 = (bf16[6,16,256]{2,1,0:T(8,128)(2,1)}, bf16[6,16,256]{2,1,0:T(8,128)(2,1)S(1)}, u32[]{:S(2)}, u32[]{:S(2)}) collective-permute-start(bf16[6,16,256]{2,1,0:T(8,128)(2,1)} %get-tuple-element.64), channel_id=1, source_target_pairs={{0,128},{64,192},{128,0},{192,64},{1,129},{65,193},{129,1},{193,65... | collective-permute-start | bytes 147464 | tf_op jit(solution)/shard_map/state_rows/ppermute | solution.py:472
  13.7 1.2 collective-permute-start.2
  14.8 1.3 norm_rows.1
  16.2 0.8 convert_element_type.33
  17.0 2.5 %fusion.11 = bf16[4,512,256]{2,1,0:T(8,128)(2,1)S(1)} fusion(bf16[1024,4,256]{2,1,0:T(4,128)(2,1)S(1)} %copy-done, bf16[1024,1024]{1,0:T(8,128)(2,1)} %param.12, s32[]{:T(128)S(6)} %select_n.38), kind=kOutput, calls=%fused_computation.8 | convolution fusion | flops 1074266112 | bytes 4194308 | tf_op jit(solution)/shard_map/grad_sum/ti,tnc->nic/dot_general | solution.py:486
  19.7 1.6 collective-permute-start.3
  21.3 2.5 %fusion.5 = f32[4,512,256]{2,1,0:T(8,128)S(1)} fusion(bf16[1024,4,256]{2,1,0:T(4,128)(2,1)S(1)} %copy-done, bf16[1024,1024]{1,0:T(8,128)(2,1)} %param.12, s32[]{:T(128)S(6)} %select_n.37), kind=kOutput, calls=%fused_computation.6 | convolution fusion | flops 1073741824 | bytes 5242884 | tf_op jit(solution)/shard_map/grad_sum/ti,tnc->nic/dot_general | solution.py:486
  23.9 2.6 %fusion.trigger = bf16[4,528,256]{2,1,0:T(8,128)(2,1)} fusion(f32[4,16,256]{2,1,0:T(8,128)S(1)} %copy-done.20, f32[4,512,256]{2,1,0:T(8,128)S(1)} %fusion.5, bf16[4,528,256]{2,1,0:T(8,128)(2,1)} %collective-permute-done.3), kind=kLoop, calls=%fused_computation.1 | loop fusion | flops 2162688 | bytes 4325376 | tf_op jit(solution)/shard_map/grad_sum/convert_element_type | solution.py:492
  26.4 1.6 spread.1
  28.1 1.3 collective-permute-start.13
  29.4 2.6 %collective-permute-start.14 = (bf16[8,16,256]{2,1,0:T(8,128)(2,1)}, bf16[8,16,256]{2,1,0:T(8,128)(2,1)S(1)}, u32[]{:S(2)}, u32[]{:S(2)}) collective-permute-start(bf16[8,16,256]{2,1,0:T(8,128)(2,1)} %get-tuple-element.79.refs_0_), channel_id=1, source_target_pairs={{0,2},{1,3},{2,0},{3,1},{4,6},{5,7},{6,4},{7,5},{8,10},{9,11},{10,... | collective-permute-start | bytes 196616 | tf_op jit(solution)/shard_map/grad_sum/ppermute | solution.py:33
  32.0 1.1 collective-permute-start.15
  33.1 2.5 %collective-permute-done.14.refs_2_ = bf16[8,16,256]{2,1,0:T(8,128)(2,1)S(1)} collective-permute-done((bf16[8,16,256]{2,1,0:T(8,128)(2,1)}, bf16[8,16,256]{2,1,0:T(8,128)(2,1)S(1)}, u32[]{:S(2)}, u32[]{:S(2)}) %collective-permute-start.14) | collective-permute-done | bytes 65568 | tf_op jit(solution)/shard_map/grad_sum/ppermute | solution.py:33
  36.2 1.7 join.3
  38.0 0.9 dynamic-slice_bitcast_fusion
  39.0 0.9 collective-permute-start.4
  39.9 2.7 %collective-permute-start.6 = (bf16[528,256]{1,0:T(8,128)(2,1)S(1)}, bf16[528,256]{1,0:T(8,128)(2,1)S(1)}, u32[]{:S(2)}, u32[]{:S(2)}) collective-permute-start(bf16[528,256]{1,0:T(8,128)(2,1)S(1)} %get-tuple-element.121), channel_id=1, source_target_pairs={{0,192},{64,0},{128,64},{192,128},{1,193},{65,1},{129,65},{193,129... | collective-permute-start | bytes 811016 | tf_op jit(solution)/shard_map/grad_sum/ppermute | solution.py:499
  46.4 1.4 stack.51.where
  47.8 7.2 %collective-permute-done.5.a2 = bf16[528,256]{1,0:T(8,128)(2,1)S(1)} collective-permute-done((bf16[528,256]{1,0:T(8,128)(2,1)}, bf16[528,256]{1,0:T(8,128)(2,1)S(1)}, u32[]{:S(2)}, u32[]{:S(2)}) %collective-permute-start.5) | collective-permute-done | bytes 270368 | tf_op jit(solution)/shard_map/grad_sum/ppermute | solution.py:499
  55.8 2.1 %sum_x.1.trigger = bf16[8,80,256]{2,1,0:T(8,128)(2,1)} custom-call(bf16[528,256]{1,0:T(8,128)(2,1)} %get-tuple-element.124.a0, bf16[528,256]{1,0:T(8,128)(2,1)} %copy-done.21, bf16[528,256]{1,0:T(8,128)(2,1)} %copy-done.22, bf16[528,256]{1,0:T(8,128)(2,1)} %copy-done.23), custom_call_target="tpu_custom_call" | custom-call | flops 1000000 | bytes 300000000 | tf_op jit(solution)/shard_map/grad_sum/sum_x/pallas_call | solution.py:503
  57.8 8.0 %all-to-all-start = ((bf16[8,80,256]{2,1,0:T(8,128)(2,1)}), bf16[8,80,256]{2,1,0:T(8,128)(2,1)S(1)}, u32[]{:S(2)}, u32[]{:S(2)}) async-start(bf16[8,80,256]{2,1,0:T(8,128)(2,1)} %sum_x.1.trigger), calls=%async_computation | async-start | bytes 655360 | tf_op jit(solution)/shard_map/grad_sum/all_to_all | solution.py:29
  65.8 0.9 collective-permute-start.7
  66.7 0.9 collective-permute-done.7.other
  68.2 1.4 choose.1
  69.6 2.7 %collective-permute-start.9 = (bf16[4,16,256]{2,1,0:T(8,128)(2,1)}, bf16[4,16,256]{2,1,0:T(8,128)(2,1)S(1)}, u32[]{:S(2)}, u32[]{:S(2)}) collective-permute-start(bf16[4,16,256]{2,1,0:T(8,128)(2,1)} %get-tuple-element.77), channel_id=1, source_target_pairs={{0,3},{1,0},{2,1},{3,2},{4,7},{5,4},{6,5},{7,6},{8,11},{9,8},{10,9... | collective-permute-start | bytes 98312 | tf_op jit(solution)/shard_map/grad_sum/ppermute | solution.py:33
  73.0 1.2 collective-permute-done.8.refs_1_
  74.2 2.9 %collective-permute-done.10.refs_3_ = bf16[4,16,256]{2,1,0:T(8,128)(2,1)S(1)} collective-permute-done((bf16[4,16,256]{2,1,0:T(8,128)(2,1)}, bf16[4,16,256]{2,1,0:T(8,128)(2,1)S(1)}, u32[]{:S(2)}, u32[]{:S(2)}) %collective-permute-start.10) | collective-permute-done | bytes 32800 | tf_op jit(solution)/shard_map/grad_sum/ppermute | solution.py:33
  77.7 1.5 join.2
  79.2 3.5 %all-to-all-done = bf16[8,80,256]{2,1,0:T(8,128)(2,1)S(1)} async-done(((bf16[8,80,256]{2,1,0:T(8,128)(2,1)}), bf16[8,80,256]{2,1,0:T(8,128)(2,1)S(1)}, u32[]{:S(2)}, u32[]{:S(2)}) %all-to-all-start) | async-done | bytes 327712 | tf_op jit(solution)/shard_map/grad_sum/all_to_all | solution.py:29
  84.2 3.4 %all-to-all-start.1 = ((bf16[8,80,256]{2,1,0:T(8,128)(2,1)}), bf16[8,80,256]{2,1,0:T(8,128)(2,1)S(1)}, u32[]{:S(2)}, u32[]{:S(2)}) async-start(bf16[8,80,256]{2,1,0:T(8,128)(2,1)} %broadcast_in_dim.39), calls=%async_computation.1 | async-start | bytes 655360 | tf_op jit(solution)/shard_map/grad_all/all_to_all | solution.py:29
  87.7 11.0 %all-to-all-done.1 = bf16[8,80,256]{2,1,0:T(8,128)(2,1)S(1)} async-done(((bf16[8,80,256]{2,1,0:T(8,128)(2,1)}), bf16[8,80,256]{2,1,0:T(8,128)(2,1)S(1)}, u32[]{:S(2)}, u32[]{:S(2)}) %all-to-all-start.1) | async-done | bytes 327712 | tf_op jit(solution)/shard_map/grad_all/all_to_all | solution.py:29
  98.8 3.2 %collective-permute-start.16 = (bf16[8,40,16,256]{3,2,1,0:T(8,128)(2,1)}, bf16[8,40,16,256]{3,2,1,0:T(8,128)(2,1)}, u32[]{:S(2)}, u32[]{:S(2)}) collective-permute-start(bf16[8,40,16,256]{3,2,1,0:T(8,128)(2,1)} %bitcast.41), channel_id=1, source_target_pairs={{0,4},{4,0},{1,5},{5,1},{2,6},{6,2},{3,7},{7,3},{8,12},{12,8},{9,1... | collective-permute-start | bytes 7864328 | tf_op jit(solution)/shard_map/grad_all/ppermute | solution.py:25
  102.1 2.7 %collective-permute-start.17 = (bf16[512,256]{1,0:T(8,128)(2,1)S(1)}, bf16[512,256]{1,0:T(8,128)(2,1)S(1)}, u32[]{:S(2)}, u32[]{:S(2)}) collective-permute-start(bf16[512,256]{1,0:T(8,128)(2,1)S(1)} %bitcast.45), channel_id=1, source_target_pairs={{0,3},{1,0},{2,1},{3,2},{4,7},{5,4},{6,5},{7,6},{8,11},{9,8},{10,9... | collective-permute-start | bytes 786440 | tf_op jit(solution)/shard_map/grad_all/ppermute | solution.py:33
  105.0 0.8 collective-permute-start.18
  105.7 5.6 %collective-permute-done.11.refs_1_ = bf16[512,256]{1,0:T(8,128)(2,1)S(1)} collective-permute-done((bf16[512,256]{1,0:T(8,128)(2,1)S(1)}, bf16[512,256]{1,0:T(8,128)(2,1)S(1)}, u32[]{:S(2)}, u32[]{:S(2)}) %collective-permute-start.11) | collective-permute-done | bytes 262176 | tf_op jit(solution)/shard_map/grad_all/ppermute | solution.py:33
  111.3 0.9 collective-permute-start.19
  112.2 3.4 %collective-permute-done.17.refs_3_ = bf16[512,256]{1,0:T(8,128)(2,1)S(1)} collective-permute-done((bf16[512,256]{1,0:T(8,128)(2,1)S(1)}, bf16[512,256]{1,0:T(8,128)(2,1)S(1)}, u32[]{:S(2)}, u32[]{:S(2)}) %collective-permute-start.17) | collective-permute-done | bytes 262176 | tf_op jit(solution)/shard_map/grad_all/ppermute | solution.py:33
  115.7 1.3 collective-permute-start.21
  116.9 1.8 copy-done.1
  118.7 2.6 %prep.1 = (bf16[1024,1024]{1,0:T(8,128)(2,1)S(1)}, bf16[1024,1024]{1,0:T(8,128)(2,1)S(1)}) custom-call(s32[9]{0:T(128)S(1)} %stack.51.where, bf16[8,40,16,256]{3,2,1,0:T(8,128)(2,1)S(1)} %bitcast.42, bf16[8,40,16,256]{3,2,1,0:T(8,128)(2,1)} %collective-permute-done.16.oth), custom_call_target="tpu_custom_call" | custom-call | tf_op jit(solution)/shard_map/grad_all/prep/pallas_call | solution.py:74
  121.5 1.5 collective-permute-done.20.refs_6_
  123.0 5.5 %rotate.1 = (bf16[1024,1024]{1,0:T(8,128)(2,1)S(1)}, bf16[1024,1024]{1,0:T(8,128)(2,1)S(1)}, bf16[4,512,256]{2,1,0:T(8,128)(2,1)S(1)}, bf16[4,16,256]{2,1,0:T(8,128)(2,1)S(1)}) custom-call(s32[9]{0:T(128)S(1)} %stack.51.where, bf16[512,256]{1,0:T(8,128)(2,1)S(1)} %bitcast.48, bf16[512,256]{1,0:T(8,128)(2,1)S(1)} %collective-permute-done.11.refs_1_, ...), custom_call_target="tpu_custom_call" | custom-call | tf_op jit(solution)/shard_map/rotate/rotate/pallas_call | solution.py:74
  128.5 1.0 copy-done.9
  129.5 1.3 copy-done.14
  130.8 1.4 copy-done.16
  132.2 4.7 %all-to-all-start.2 = ((bf16[4,512,256]{2,1,0:T(8,128)(2,1)}), bf16[4,512,256]{2,1,0:T(8,128)(2,1)S(1)}, u32[]{:S(2)}, u32[]{:S(2)}) async-start(bf16[4,512,256]{2,1,0:T(8,128)(2,1)} %copy-done.9), calls=%async_computation.2 | async-start | bytes 2097152 | tf_op jit(solution)/shard_map/rotate/all_to_all | solution.py:29
  136.8 1.6 copy-done.4
  138.4 1.6 copy-done.7
  140.0 1.3 copy-done.18
  141.3 3.0 %old_power.1.old = f32[1024,1024]{1,0:T(8,128)S(1)} custom-call(s32[9]{0:T(128)S(1)} %stack.51.where, bf16[8,20,16,256]{3,2,1,0:T(8,128)(2,1)S(1)} %bitcast.49, bf16[1024,1024]{1,0:T(8,128)(2,1)S(1)} %copy-done.4, bf16[1024,1024]{1,0:T(8,128)(2,1)S(1)} %copy-done.7), custom_call_target="tpu_custom_call" | custom-call | flops 6000000000 | bytes 24000000 | tf_op jit(solution)/shard_map/power/old_power/pallas_call | solution.py:74
  144.4 6.9 %power.1 = (bf16[4,32,256]{2,1,0:T(8,128)(2,1)S(1)}, bf16[4,32,256]{2,1,0:T(8,128)(2,1)S(1)}) custom-call(s32[9]{0:T(128)S(1)} %stack.51.where, bf16[1024,1024]{1,0:T(8,128)(2,1)S(1)} %copy-done.15, bf16[1024,1024]{1,0:T(8,128)(2,1)S(1)} %copy-done.17, f32[1024,1024]{1,0:T(8,128)S(1)} %old_power.1.old), custom_call_target="tpu_custom_call" | custom-call | flops 6000000000 | bytes 24000000 | tf_op jit(solution)/shard_map/power/power/pallas_call | solution.py:74
  151.3 0.8 all-to-all-done.2.direct
  152.1 1.7 copy-done.8
  153.8 1.0 back.1.own
  155.4 1.2 collective-permute-done.22.oth
  156.5 1.2 update.1
  158.0 1.2 collective-permute-start.24
  159.3 1.5 collective-permute-start.25
  160.8 13.5 %collective-permute-done.23.g1 = bf16[608,256]{1,0:T(8,128)(2,1)S(1)} collective-permute-done((bf16[608,256]{1,0:T(8,128)(2,1)S(1)}, bf16[608,256]{1,0:T(8,128)(2,1)S(1)}, u32[]{:S(2)}, u32[]{:S(2)}) %collective-permute-start.23) | collective-permute-done | bytes 311328 | tf_op jit(solution)/shard_map/home/ppermute | solution.py:37
  175.3 1.6 collective-permute-start.26
  176.9 1.3 collective-permute-done.26.recv
  178.2 1.5 final.1
  (118 shorter events, 9.9 us)
Async XLA Ops:
  7.2 9.8 %copy-start = (bf16[1024,4,256]{2,1,0:T(4,128)(2,1)S(1)}, bf16[1024,4,256]{2,1,0:T(4,128)(2,1)}, u32[]{:S(2)}) copy-start(bf16[1024,4,256]{2,1,0:T(4,128)(2,1)} %param.13) | copy-start | bytes 6291460
  7.2 91.6 %all-gather.5.cloned.1.call-start = ((), (), s32[]{:S(2)}) async-start(), calls=%async_computation.3 | async-start | bytes 2949120 | tf_op jit(solution)/shard_map/grad_sum/all_gather | solution.py:496
  9.1 10.5 %collective-permute-start = (bf16[6,16,256]{2,1,0:T(8,128)(2,1)}, bf16[6,16,256]{2,1,0:T(8,128)(2,1)S(1)}, u32[]{:S(2)}, u32[]{:S(2)}) collective-permute-start(bf16[6,16,256]{2,1,0:T(8,128)(2,1)} %get-tuple-element.63), channel_id=1, source_target_pairs={{0,64},{64,128},{128,192},{192,0},{1,65},{65,129},{129,193},{193,1... | collective-permute-start | bytes 147464 | tf_op jit(solution)/shard_map/state_rows/ppermute | solution.py:472
  11.2 8.4 %collective-permute-start.1 = (bf16[6,16,256]{2,1,0:T(8,128)(2,1)}, bf16[6,16,256]{2,1,0:T(8,128)(2,1)S(1)}, u32[]{:S(2)}, u32[]{:S(2)}) collective-permute-start(bf16[6,16,256]{2,1,0:T(8,128)(2,1)} %get-tuple-element.64), channel_id=1, source_target_pairs={{0,128},{64,192},{128,0},{192,64},{1,129},{65,193},{129,1},{193,65... | collective-permute-start | bytes 147464 | tf_op jit(solution)/shard_map/state_rows/ppermute | solution.py:472
  13.7 6.0 %collective-permute-start.2 = (bf16[6,16,256]{2,1,0:T(8,128)(2,1)}, bf16[6,16,256]{2,1,0:T(8,128)(2,1)S(1)}, u32[]{:S(2)}, u32[]{:S(2)}) collective-permute-start(bf16[6,16,256]{2,1,0:T(8,128)(2,1)} %get-tuple-element.65), channel_id=1, source_target_pairs={{0,192},{64,0},{128,64},{192,128},{1,193},{65,1},{129,65},{193,129... | collective-permute-start | bytes 147464 | tf_op jit(solution)/shard_map/state_rows/ppermute | solution.py:472
  19.6 4.2 %copy-start.27 = (bf16[6,16,256]{2,1,0:T(8,128)(2,1)}, bf16[6,16,256]{2,1,0:T(8,128)(2,1)S(1)}, u32[]{:S(2)}) copy-start(bf16[6,16,256]{2,1,0:T(8,128)(2,1)S(1)} %collective-permute-done.r1) | copy-start | bytes 147460
  19.6 4.2 %copy-start.28 = (bf16[6,16,256]{2,1,0:T(8,128)(2,1)}, bf16[6,16,256]{2,1,0:T(8,128)(2,1)S(1)}, u32[]{:S(2)}) copy-start(bf16[6,16,256]{2,1,0:T(8,128)(2,1)S(1)} %collective-permute-done.1.r2) | copy-start | bytes 147460
  19.7 4.2 %copy-start.29 = (bf16[6,16,256]{2,1,0:T(8,128)(2,1)}, bf16[6,16,256]{2,1,0:T(8,128)(2,1)S(1)}, u32[]{:S(2)}) copy-start(bf16[6,16,256]{2,1,0:T(8,128)(2,1)S(1)} %collective-permute-done.2.r3) | copy-start | bytes 147460
  19.7 4.2 %collective-permute-start.3 = (bf16[4,528,256]{2,1,0:T(8,128)(2,1)S(1)}, bf16[4,528,256]{2,1,0:T(8,128)(2,1)}, u32[]{:S(2)}, u32[]{:S(2)}) collective-permute-start(bf16[4,528,256]{2,1,0:T(8,128)(2,1)S(1)} %pad_maximum_fusion), channel_id=1, source_target_pairs={{0,4},{4,0},{1,5},{5,1},{2,6},{6,2},{3,7},{7,3},{8,12},{12,8},{9,1... | collective-permute-start | bytes 3244040 | tf_op jit(solution)/shard_map/grad_sum/ppermute | solution.py:25
  21.3 2.6 %copy-start.20 = (f32[4,16,256]{2,1,0:T(8,128)S(1)}, f32[4,16,256]{2,1,0:T(8,128)}, u32[]{:S(2)}) copy-start(f32[4,16,256]{2,1,0:T(8,128)} %norm_rows.1) | copy-start | bytes 196612
  26.4 11.6 %copy-start.19 = (bf16[4,528,256]{2,1,0:T(8,128)(2,1)S(1)}, bf16[4,528,256]{2,1,0:T(8,128)(2,1)}, u32[]{:S(2)}) copy-start(bf16[4,528,256]{2,1,0:T(8,128)(2,1)} %fusion.trigger) | copy-start | bytes 3244036
  26.4 16.1 %copy-start.34 = (s32[5]{0:T(128)S(1)}, s32[5]{0:T(128)}, u32[]{:S(2)}) copy-start(s32[5]{0:T(128)} %param.15) | copy-start | bytes 64
  28.1 5.0 %collective-permute-start.13 = (bf16[8,16,256]{2,1,0:T(8,128)(2,1)}, bf16[8,16,256]{2,1,0:T(8,128)(2,1)S(1)}, u32[]{:S(2)}, u32[]{:S(2)}) collective-permute-start(bf16[8,16,256]{2,1,0:T(8,128)(2,1)} %get-tuple-element.79.refs_0_), channel_id=1, source_target_pairs={{0,1},{1,2},{2,3},{3,0},{4,5},{5,6},{6,7},{7,4},{8,9},{9,10},{10,1... | collective-permute-start | bytes 196616 | tf_op jit(solution)/shard_map/grad_sum/ppermute | solution.py:33
  29.4 6.2 %collective-permute-start.14 = (bf16[8,16,256]{2,1,0:T(8,128)(2,1)}, bf16[8,16,256]{2,1,0:T(8,128)(2,1)S(1)}, u32[]{:S(2)}, u32[]{:S(2)}) collective-permute-start(bf16[8,16,256]{2,1,0:T(8,128)(2,1)} %get-tuple-element.79.refs_0_), channel_id=1, source_target_pairs={{0,2},{1,3},{2,0},{3,1},{4,6},{5,7},{6,4},{7,5},{8,10},{9,11},{10,... | collective-permute-start | bytes 196616 | tf_op jit(solution)/shard_map/grad_sum/ppermute | solution.py:33
  32.0 3.6 %collective-permute-start.15 = (bf16[8,16,256]{2,1,0:T(8,128)(2,1)}, bf16[8,16,256]{2,1,0:T(8,128)(2,1)S(1)}, u32[]{:S(2)}, u32[]{:S(2)}) collective-permute-start(bf16[8,16,256]{2,1,0:T(8,128)(2,1)} %get-tuple-element.79.refs_0_), channel_id=1, source_target_pairs={{0,3},{1,0},{2,1},{3,2},{4,7},{5,4},{6,5},{7,6},{8,11},{9,8},{10,9... | collective-permute-start | bytes 196616 | tf_op jit(solution)/shard_map/grad_sum/ppermute | solution.py:33
  33.1 2.6 %copy-start.24 = (bf16[8,16,256]{2,1,0:T(8,128)(2,1)}, bf16[8,16,256]{2,1,0:T(8,128)(2,1)S(1)}, u32[]{:S(2)}) copy-start(bf16[8,16,256]{2,1,0:T(8,128)(2,1)S(1)} %collective-permute-done.13.refs_1_) | copy-start | bytes 196612
  38.0 27.8 %copy-start.37 = (bf16[4,16,256]{2,1,0:T(8,128)(2,1)S(1)}, bf16[4,16,256]{2,1,0:T(8,128)(2,1)}, u32[]{:S(2)}) copy-start(bf16[4,16,256]{2,1,0:T(8,128)(2,1)} %get-tuple-element.74) | copy-start | bytes 98308
  38.9 43.8 %copy-start.35 = (f32[32]{0:T(128)S(1)}, f32[32]{0:T(128)}, u32[]{:S(2)}) copy-start(f32[32]{0:T(128)} %param.22) | copy-start | bytes 388
  38.9 43.8 %copy-start.36 = (f32[32]{0:T(128)S(1)}, f32[32]{0:T(128)}, u32[]{:S(2)}) copy-start(f32[32]{0:T(128)} %param.23) | copy-start | bytes 388
  39.0 8.8 %collective-permute-start.4 = (bf16[528,256]{1,0:T(8,128)(2,1)}, bf16[528,256]{1,0:T(8,128)(2,1)S(1)}, u32[]{:S(2)}, u32[]{:S(2)}) collective-permute-start(bf16[528,256]{1,0:T(8,128)(2,1)} %get-tuple-element.123), channel_id=1, source_target_pairs={{0,128},{64,192},{128,0},{192,64},{1,129},{65,193},{129,1},{193,65... | collective-permute-start | bytes 811016 | tf_op jit(solution)/shard_map/grad_sum/ppermute | solution.py:499
  39.9 15.1 %collective-permute-start.5 = (bf16[528,256]{1,0:T(8,128)(2,1)}, bf16[528,256]{1,0:T(8,128)(2,1)S(1)}, u32[]{:S(2)}, u32[]{:S(2)}) collective-permute-start(bf16[528,256]{1,0:T(8,128)(2,1)} %get-tuple-element.122), channel_id=1, source_target_pairs={{0,64},{64,128},{128,192},{192,0},{1,65},{65,129},{129,193},{193,1... | collective-permute-start | bytes 811016 | tf_op jit(solution)/shard_map/grad_sum/ppermute | solution.py:499
  39.9 15.1 %collective-permute-start.6 = (bf16[528,256]{1,0:T(8,128)(2,1)S(1)}, bf16[528,256]{1,0:T(8,128)(2,1)S(1)}, u32[]{:S(2)}, u32[]{:S(2)}) collective-permute-start(bf16[528,256]{1,0:T(8,128)(2,1)S(1)} %get-tuple-element.121), channel_id=1, source_target_pairs={{0,192},{64,0},{128,64},{192,128},{1,193},{65,1},{129,65},{193,129... | collective-permute-start | bytes 811016 | tf_op jit(solution)/shard_map/grad_sum/ppermute | solution.py:499
  47.8 7.2 %copy-start.21 = (bf16[528,256]{1,0:T(8,128)(2,1)}, bf16[528,256]{1,0:T(8,128)(2,1)S(1)}, u32[]{:S(2)}) copy-start(bf16[528,256]{1,0:T(8,128)(2,1)S(1)} %collective-permute-done.4.a1) | copy-start | bytes 811012
  57.8 24.9 %all-to-all-start = ((bf16[8,80,256]{2,1,0:T(8,128)(2,1)}), bf16[8,80,256]{2,1,0:T(8,128)(2,1)S(1)}, u32[]{:S(2)}, u32[]{:S(2)}) async-start(bf16[8,80,256]{2,1,0:T(8,128)(2,1)} %sum_x.1.trigger), calls=%async_computation | async-start | bytes 655360 | tf_op jit(solution)/shard_map/grad_sum/all_to_all | solution.py:29
  65.8 1.8 collective-permute-start.7
  69.6 4.6 %collective-permute-start.8 = (bf16[4,16,256]{2,1,0:T(8,128)(2,1)}, bf16[4,16,256]{2,1,0:T(8,128)(2,1)S(1)}, u32[]{:S(2)}, u32[]{:S(2)}) collective-permute-start(bf16[4,16,256]{2,1,0:T(8,128)(2,1)} %get-tuple-element.76), channel_id=1, source_target_pairs={{0,1},{1,2},{2,3},{3,0},{4,5},{5,6},{6,7},{7,4},{8,9},{9,10},{10,1... | collective-permute-start | bytes 98312 | tf_op jit(solution)/shard_map/grad_sum/ppermute | solution.py:33
  69.6 4.6 %collective-permute-start.9 = (bf16[4,16,256]{2,1,0:T(8,128)(2,1)}, bf16[4,16,256]{2,1,0:T(8,128)(2,1)S(1)}, u32[]{:S(2)}, u32[]{:S(2)}) collective-permute-start(bf16[4,16,256]{2,1,0:T(8,128)(2,1)} %get-tuple-element.77), channel_id=1, source_target_pairs={{0,3},{1,0},{2,1},{3,2},{4,7},{5,4},{6,5},{7,6},{8,11},{9,8},{10,9... | collective-permute-start | bytes 98312 | tf_op jit(solution)/shard_map/grad_sum/ppermute | solution.py:33
  72.3 4.8 %collective-permute-start.10 = (bf16[4,16,256]{2,1,0:T(8,128)(2,1)}, bf16[4,16,256]{2,1,0:T(8,128)(2,1)S(1)}, u32[]{:S(2)}, u32[]{:S(2)}) collective-permute-start(bf16[4,16,256]{2,1,0:T(8,128)(2,1)} %get-tuple-element.77), channel_id=1, source_target_pairs={{0,2},{1,3},{2,0},{3,1},{4,6},{5,7},{6,4},{7,5},{8,10},{9,11},{10,... | collective-permute-start | bytes 98312 | tf_op jit(solution)/shard_map/grad_sum/ppermute | solution.py:33
  74.2 2.9 %copy-start.30 = (bf16[4,16,256]{2,1,0:T(8,128)(2,1)}, bf16[4,16,256]{2,1,0:T(8,128)(2,1)S(1)}, u32[]{:S(2)}) copy-start(bf16[4,16,256]{2,1,0:T(8,128)(2,1)S(1)} %collective-permute-done.8.refs_1_) | copy-start | bytes 98308
  74.2 2.9 %copy-start.31 = (bf16[4,16,256]{2,1,0:T(8,128)(2,1)}, bf16[4,16,256]{2,1,0:T(8,128)(2,1)S(1)}, u32[]{:S(2)}) copy-start(bf16[4,16,256]{2,1,0:T(8,128)(2,1)S(1)} %collective-permute-done.9.refs_2_) | copy-start | bytes 98308
  84.2 14.5 %all-to-all-start.1 = ((bf16[8,80,256]{2,1,0:T(8,128)(2,1)}), bf16[8,80,256]{2,1,0:T(8,128)(2,1)S(1)}, u32[]{:S(2)}, u32[]{:S(2)}) async-start(bf16[8,80,256]{2,1,0:T(8,128)(2,1)} %broadcast_in_dim.39), calls=%async_computation.1 | async-start | bytes 655360 | tf_op jit(solution)/shard_map/grad_all/all_to_all | solution.py:29
  87.6 49.2 %all-gather.7.cloned.1.call-start = ((), (), s32[]{:S(2)}) async-start(), calls=%async_computation.4 | async-start | bytes 1474560 | tf_op jit(solution)/shard_map/grad_sum/all_gather | solution.py:518
  98.8 18.1 %collective-permute-start.16 = (bf16[8,40,16,256]{3,2,1,0:T(8,128)(2,1)}, bf16[8,40,16,256]{3,2,1,0:T(8,128)(2,1)}, u32[]{:S(2)}, u32[]{:S(2)}) collective-permute-start(bf16[8,40,16,256]{3,2,1,0:T(8,128)(2,1)} %bitcast.41), channel_id=1, source_target_pairs={{0,4},{4,0},{1,5},{5,1},{2,6},{6,2},{3,7},{7,3},{8,12},{12,8},{9,1... | collective-permute-start | bytes 7864328 | tf_op jit(solution)/shard_map/grad_all/ppermute | solution.py:25
  102.0 9.3 %collective-permute-start.11 = (bf16[512,256]{1,0:T(8,128)(2,1)S(1)}, bf16[512,256]{1,0:T(8,128)(2,1)S(1)}, u32[]{:S(2)}, u32[]{:S(2)}) collective-permute-start(bf16[512,256]{1,0:T(8,128)(2,1)S(1)} %bitcast.44), channel_id=1, source_target_pairs={{0,1},{1,2},{2,3},{3,0},{4,5},{5,6},{6,7},{7,4},{8,9},{9,10},{10,1... | collective-permute-start | bytes 786440 | tf_op jit(solution)/shard_map/grad_all/ppermute | solution.py:33
  102.1 13.5 %collective-permute-start.17 = (bf16[512,256]{1,0:T(8,128)(2,1)S(1)}, bf16[512,256]{1,0:T(8,128)(2,1)S(1)}, u32[]{:S(2)}, u32[]{:S(2)}) collective-permute-start(bf16[512,256]{1,0:T(8,128)(2,1)S(1)} %bitcast.45), channel_id=1, source_target_pairs={{0,3},{1,0},{2,1},{3,2},{4,7},{5,4},{6,5},{7,6},{8,11},{9,8},{10,9... | collective-permute-start | bytes 786440 | tf_op jit(solution)/shard_map/grad_all/ppermute | solution.py:33
  104.8 16.6 %collective-permute-start.12 = (bf16[512,256]{1,0:T(8,128)(2,1)S(1)}, bf16[512,256]{1,0:T(8,128)(2,1)S(1)}, u32[]{:S(2)}, u32[]{:S(2)}) collective-permute-start(bf16[512,256]{1,0:T(8,128)(2,1)S(1)} %bitcast.46), channel_id=1, source_target_pairs={{0,2},{1,3},{2,0},{3,1},{4,6},{5,7},{6,4},{7,5},{8,10},{9,11},{10,... | collective-permute-start | bytes 786440 | tf_op jit(solution)/shard_map/grad_all/ppermute | solution.py:33
  105.0 16.5 %collective-permute-start.18 = (bf16[512,256]{1,0:T(8,128)(2,1)S(1)}, bf16[512,256]{1,0:T(8,128)(2,1)S(1)}, u32[]{:S(2)}, u32[]{:S(2)}) collective-permute-start(bf16[512,256]{1,0:T(8,128)(2,1)S(1)} %bitcast.47), channel_id=1, source_target_pairs={{0,4},{4,0},{1,5},{5,1},{2,6},{6,2},{3,7},{7,3},{8,12},{12,8},{9,1... | collective-permute-start | bytes 786440 | tf_op jit(solution)/shard_map/grad_all/ppermute | solution.py:25
  111.3 10.1 %collective-permute-start.19 = (bf16[512,256]{1,0:T(8,128)(2,1)S(1)}, bf16[512,256]{1,0:T(8,128)(2,1)S(1)}, u32[]{:S(2)}, u32[]{:S(2)}) collective-permute-start(bf16[512,256]{1,0:T(8,128)(2,1)S(1)} %collective-permute-done.11.refs_1_), channel_id=1, source_target_pairs={{0,4},{4,0},{1,5},{5,1},{2,6},{6,2},{3,7},{7,3},{8,12},{12,8},{9,1... | collective-permute-start | bytes 786440 | tf_op jit(solution)/shard_map/grad_all/ppermute | solution.py:25
  115.7 5.8 %collective-permute-start.21 = (bf16[512,256]{1,0:T(8,128)(2,1)S(1)}, bf16[512,256]{1,0:T(8,128)(2,1)S(1)}, u32[]{:S(2)}, u32[]{:S(2)}) collective-permute-start(bf16[512,256]{1,0:T(8,128)(2,1)S(1)} %collective-permute-done.17.refs_3_), channel_id=1, source_target_pairs={{0,4},{4,0},{1,5},{5,1},{2,6},{6,2},{3,7},{7,3},{8,12},{12,8},{9,1... | collective-permute-start | bytes 786440 | tf_op jit(solution)/shard_map/grad_all/ppermute | solution.py:25
  116.9 1.8 copy-start.1
  118.7 4.3 %copy-start.2 = (bf16[320,16,256]{2,1,0:T(8,128)(2,1)S(1)}, bf16[320,16,256]{2,1,0:T(8,128)(2,1)}, u32[]{:S(2)}) copy-start(bf16[320,16,256]{2,1,0:T(8,128)(2,1)} %all-gather.5.cloned.1.call-done) | copy-start | bytes 7864324
  121.3 7.2 %copy-start.3 = (bf16[1024,1024]{1,0:T(8,128)(2,1)}, bf16[1024,1024]{1,0:T(8,128)(2,1)S(1)}, u32[]{:S(2)}) copy-start(bf16[1024,1024]{1,0:T(8,128)(2,1)S(1)} %get-tuple-element.85.refs_8_.left) | copy-start | bytes 6291460
  121.3 7.2 %copy-start.6 = (bf16[1024,1024]{1,0:T(8,128)(2,1)}, bf16[1024,1024]{1,0:T(8,128)(2,1)S(1)}, u32[]{:S(2)}) copy-start(bf16[1024,1024]{1,0:T(8,128)(2,1)S(1)} %get-tuple-element.86.refs_9_.right) | copy-start | bytes 6291460
  121.3 1.6 collective-permute-start.20
  128.5 1.0 copy-start.9
  129.5 1.3 copy-start.14
  130.8 1.4 copy-start.16
  132.2 19.9 %all-to-all-start.2 = ((bf16[4,512,256]{2,1,0:T(8,128)(2,1)}), bf16[4,512,256]{2,1,0:T(8,128)(2,1)S(1)}, u32[]{:S(2)}, u32[]{:S(2)}) async-start(bf16[4,512,256]{2,1,0:T(8,128)(2,1)} %copy-done.9), calls=%async_computation.2 | async-start | bytes 2097152 | tf_op jit(solution)/shard_map/rotate/all_to_all | solution.py:29
  136.8 1.6 copy-start.4
  138.4 1.6 copy-start.7
  140.0 1.3 copy-start.18
  141.3 3.0 %copy-start.15 = (bf16[1024,1024]{1,0:T(8,128)(2,1)S(1)}, bf16[1024,1024]{1,0:T(8,128)(2,1)}, u32[]{:S(2)}) copy-start(bf16[1024,1024]{1,0:T(8,128)(2,1)} %copy-done.14) | copy-start | bytes 6291460
  141.3 3.0 %copy-start.17 = (bf16[1024,1024]{1,0:T(8,128)(2,1)S(1)}, bf16[1024,1024]{1,0:T(8,128)(2,1)}, u32[]{:S(2)}) copy-start(bf16[1024,1024]{1,0:T(8,128)(2,1)} %copy-done.16) | copy-start | bytes 6291460
  152.1 4.5 %copy-start.5 = (bf16[1024,1024]{1,0:T(8,128)(2,1)S(1)}, bf16[1024,1024]{1,0:T(8,128)(2,1)}, u32[]{:S(2)}) copy-start(bf16[1024,1024]{1,0:T(8,128)(2,1)} %copy-done.3) | copy-start | bytes 6291460
  152.1 1.7 copy-start.8
  154.8 23.3 %copy-start.10 = (f32[4,16,256]{2,1,0:T(8,128)S(1)}, f32[4,16,256]{2,1,0:T(8,128)}, u32[]{:S(2)}) copy-start(f32[4,16,256]{2,1,0:T(8,128)} %m1.1) | copy-start | bytes 196612
  154.8 23.3 %copy-start.11 = (f32[4,16,256]{2,1,0:T(8,128)S(1)}, f32[4,16,256]{2,1,0:T(8,128)}, u32[]{:S(2)}) copy-start(f32[4,16,256]{2,1,0:T(8,128)} %m2.1) | copy-start | bytes 196612
  154.8 23.3 %copy-start.12 = (f32[4,16,256]{2,1,0:T(8,128)S(1)}, f32[4,16,256]{2,1,0:T(8,128)}, u32[]{:S(2)}) copy-start(f32[4,16,256]{2,1,0:T(8,128)} %sl.1) | copy-start | bytes 196612
  154.9 23.3 %copy-start.13 = (f32[4,16,256]{2,1,0:T(8,128)S(1)}, f32[4,16,256]{2,1,0:T(8,128)}, u32[]{:S(2)}) copy-start(f32[4,16,256]{2,1,0:T(8,128)} %sr.1) | copy-start | bytes 196612
  154.9 1.6 collective-permute-start.22
  157.8 16.5 %collective-permute-start.23 = (bf16[608,256]{1,0:T(8,128)(2,1)S(1)}, bf16[608,256]{1,0:T(8,128)(2,1)S(1)}, u32[]{:S(2)}, u32[]{:S(2)}) collective-permute-start(bf16[608,256]{1,0:T(8,128)(2,1)S(1)} %get-tuple-element.101), channel_id=1, source_target_pairs={{0,64},{64,128},{128,192},{192,0},{1,65},{65,129},{129,193},{193,1... | collective-permute-start | bytes 933896 | tf_op jit(solution)/shard_map/home/ppermute | solution.py:37
  158.0 16.3 %collective-permute-start.24 = (bf16[608,256]{1,0:T(8,128)(2,1)S(1)}, bf16[608,256]{1,0:T(8,128)(2,1)S(1)}, u32[]{:S(2)}, u32[]{:S(2)}) collective-permute-start(bf16[608,256]{1,0:T(8,128)(2,1)S(1)} %get-tuple-element.102), channel_id=1, source_target_pairs={{0,128},{64,192},{128,0},{192,64},{1,129},{65,193},{129,1},{193,65... | collective-permute-start | bytes 933896 | tf_op jit(solution)/shard_map/home/ppermute | solution.py:37
  159.3 15.4 %collective-permute-start.25 = (bf16[608,256]{1,0:T(8,128)(2,1)S(1)}, bf16[608,256]{1,0:T(8,128)(2,1)S(1)}, u32[]{:S(2)}, u32[]{:S(2)}) collective-permute-start(bf16[608,256]{1,0:T(8,128)(2,1)S(1)} %get-tuple-element.103), channel_id=1, source_target_pairs={{0,192},{64,0},{128,64},{192,128},{1,193},{65,1},{129,65},{193,129... | collective-permute-start | bytes 933896 | tf_op jit(solution)/shard_map/home/ppermute | solution.py:37
  175.3 2.9 %collective-permute-start.26 = (bf16[704,256]{1,0:T(8,128)(2,1)S(1)}, bf16[704,256]{1,0:T(8,128)(2,1)S(1)}, u32[]{:S(2)}, u32[]{:S(2)}) collective-permute-start(bf16[704,256]{1,0:T(8,128)(2,1)S(1)} %get-tuple-element.105), channel_id=1, source_target_pairs={{0,4},{4,0},{1,5},{5,1},{2,6},{6,2},{3,7},{7,3},{8,12},{12,8},{9,1... | collective-permute-start | bytes 1081352 | tf_op jit(solution)/shard_map/home/ppermute | solution.py:25
  (6 other events, 4.0 us)
Sparse Core Ops, SparseCore 0:
  38.1 47.5 all-gather.4
  102.1 27.8 all-gather.6

commit v2 on v0

--- a/solution.py
+++ b/solution.py
@@ -229,7 +229,7 @@
 
 def rotate_kernel(where, *refs):
     own, oth = refs[:NM], refs[NM : 2 * NM]
-    left, right, pack, grad, work, direct, rot_home, rot = refs[2 * NM :]
+    left, right, pack, grad_out, work_out, direct, rot_home, rot, grad, work, sems = refs[2 * NM :]
     z, c, m = where[1], where[2], where[3]
     half = own[0].shape[0]
     for pieces, core in ((own, c), (oth, 1 - c)):
@@ -237,6 +237,9 @@
         for s in range(NM):
             grad[r, pl.ds(block_start(lax.rem(m - s + NM, NM), W), W)] = pieces[s][...]
     col = pl.ds(block_start(m, W), W)
+    grad_copy = pltpu.make_async_copy(grad, grad_out, sems.at[0])
+    work_copy = pltpu.make_async_copy(work, work_out, sems.at[1])
+    grad_copy.start()
 
     @pl.when(c == 0)
     def _():
@@ -248,6 +251,7 @@
         work[...] = dot_nn(grad[...], right[...]).astype(BF)
         rot[...] = dot_tn(left[...], work[:, col])
 
+    work_copy.start()
     for xp in range(NX):
         shift = shift_of(where, xp)
         for zp in range(NZ):
@@ -261,6 +265,8 @@
     for xp in range(NX):
         row = pl.multiple_of(xp * (NZ * NC * B) + z * (NC * B) + c * B, B)
         rot_home[xp] = rot[pl.ds(row, B), :].astype(BF)
+    grad_copy.wait()
+    work_copy.wait()
 
 
 def power_kernel(where, grad, work, old, outer, basis, power, iterate):
@@ -535,23 +541,26 @@
         grad_other = [swap_cores(piece) for piece in grad_own]
 
     with jax.named_scope("rotate"):
-        grad, work, direction, rot_home = call(
+        any_space = pl.BlockSpec(memory_space=pl.ANY)
+        grad, work, direction, rot_home = pl.pallas_call(
             rotate_kernel,
-            "rotate",
-            [
-                ((full, full), BF),
-                ((full, full), BF),
-                ((NM, half, W), BF),
-                ((NX, B, W), BF),
+            out_shape=[
+                jax.ShapeDtypeStruct((full, full), BF),
+                jax.ShapeDtypeStruct((full, full), BF),
+                jax.ShapeDtypeStruct((NM, half, W), BF),
+                jax.ShapeDtypeStruct((NX, B, W), BF),
             ],
-            [((full, W), F32)],
-            where,
-            *grad_own,
-            *grad_other,
-            left,
-            right,
-            pack,
-        )
+            in_specs=[SMEM] + [VMEM] * (2 * NM + 3),
+            out_specs=[any_space, any_space, VMEM, VMEM],
+            scratch_shapes=[
+                pltpu.VMEM((full, W), F32),
+                pltpu.VMEM((full, full), BF),
+                pltpu.VMEM((full, full), BF),
+                pltpu.SemaphoreType.DMA((2,)),
+            ],
+            compiler_params=pltpu.CompilerParams(vmem_limit_bytes=24 * 1024 * 1024),
+            name="rotate",
+        )(where, *grad_own, *grad_other, left, right, pack)
         stats, rot_home = lax.optimization_barrier((stats, rot_home))
         direction = exchange(direction, "mp")
     with jax.named_scope("power"):

time: 188 us -> 188 us (level)
    pallas_call x0 -> x1, Pallas kernels: none -> 5.86 us  [shards(): pl.pallas_call(rotate_kernel, out_shape=[jax.ShapeDtypeStruct((full, full...]
    pallas_call x8 -> x7, Pallas kernels: 22.5 us -> 16.9 us  [call(): pl.pallas_call(kernel, out_shape=[jax.ShapeDtypeStruct(s, d) for s, d in...]
  transfers between devices with their start and end apart: 32 -> 32, of which waited for: 17 -> 17; matrix products, arithmetic and copies ran while one was open for 7% -> 7% of each run, Pallas kernels for 12% -> 13%
where the time goes in v2:
time: 188 us; the launch traced here: 187 us
  waiting for transfers between devices  55.5 us (30%)
  starting transfers between devices  51.6 us (27%)
  Pallas kernels  33.1 us (18%)
  local copies, waits for them, and re-layouts  19.2 us (10%)
  between operations  16.5 us (9%)
  other arithmetic  6.03 us (3%)
  matrix products  4.99 us (3%)
    pallas_call x7, Pallas kernels, call(): pl.pallas_call(kernel, out_shape=[jax.ShapeDtypeStruct(s, d) for s, d in...  16.9 us
    all_to_all x3, starting transfers between devices, exchange(): return lax.all_to_all(value, axis, 0, 0, tiled=True)  16.7 us
    unnamed x78, local copies, waits for them, and re-layouts  14.9 us
    all_to_all x3, waiting for transfers between devices, exchange(): return lax.all_to_all(value, axis, 0, 0, tiled=True)  14.1 us
    ppermute x3, waiting for transfers between devices, turn_x(): return lax.ppermute(value, 'x', [(i, (i + s) % NX) for i in range(NX)])  13.9 us
    ppermute x3, waiting for transfers between devices, shards(): lax.ppermute(tile(s), 'x', [(i, (i + s) % NX) for i in range(NX)])  12.1 us
    ppermute x9, starting transfers between devices, turn(): return lax.ppermute(value, 'mp', [(i, (i + s) % NM) for i in range(NM)])  11.6 us
    ppermute x9, starting transfers between devices, swap_cores(): return lax.ppermute(value, 'c', [(0, 1), (1, 0)])  11 us
  transfers between devices with their start and end apart: 32, of which 17 were waited for; matrix products, arithmetic and copies ran while one was open for 7% of the time, Pallas kernels for 13%

profile of v2, /device:TPU:1, one launch (start us, length us, event | category | flops | bytes accessed | tf_op | source)
XLA Modules:
  0.0 186.9 jit_solution(18209099398953425870)
XLA Ops:
  7.2 1.9 %pack.1 = (bf16[6,16,256]{2,1,0:T(8,128)(2,1)}, bf16[6,16,256]{2,1,0:T(8,128)(2,1)}, bf16[6,16,256]{2,1,0:T(8,128)(2,1)}, bf16[6,16,256]{2,1,0:T(8,128)(2,1)}) custom-call(f32[4,16,256]{2,1,0:T(8,128)} %refs_0_.1, f32[4,16,256]{2,1,0:T(8,128)} %refs_1_.1, f32[4,16,256]{2,1,0:T(8,128)} %m1.1, f32[4,16,256]{2,1,0:T(8,128)} %m2.1, f32[4,16,256]{2,1,0:T(8,128)} %sl.1, ...), custom_call_target="tpu_custom_call" | custom-call | tf_op jit(solution)/shard_map/state_rows/pack/pallas_call | solution.py:463
  9.1 2.1 %collective-permute-start = (bf16[6,16,256]{2,1,0:T(8,128)(2,1)}, bf16[6,16,256]{2,1,0:T(8,128)(2,1)S(1)}, u32[]{:S(2)}, u32[]{:S(2)}) collective-permute-start(bf16[6,16,256]{2,1,0:T(8,128)(2,1)} %get-tuple-element.61), channel_id=1, source_target_pairs={{0,64},{64,128},{128,192},{192,0},{1,65},{65,129},{129,193},{193,1... | collective-permute-start | bytes 147464 | tf_op jit(solution)/shard_map/state_rows/ppermute | solution.py:472
  11.2 2.5 %collective-permute-start.1 = (bf16[6,16,256]{2,1,0:T(8,128)(2,1)}, bf16[6,16,256]{2,1,0:T(8,128)(2,1)S(1)}, u32[]{:S(2)}, u32[]{:S(2)}) collective-permute-start(bf16[6,16,256]{2,1,0:T(8,128)(2,1)} %get-tuple-element.62), channel_id=1, source_target_pairs={{0,128},{64,192},{128,0},{192,64},{1,129},{65,193},{129,1},{193,65... | collective-permute-start | bytes 147464 | tf_op jit(solution)/shard_map/state_rows/ppermute | solution.py:472
  13.7 1.2 collective-permute-start.2
  15.4 1.4 reduce.3
  16.8 2.5 %fusion.11 = bf16[4,512,256]{2,1,0:T(8,128)(2,1)S(1)} fusion(bf16[1024,4,256]{2,1,0:T(4,128)(2,1)S(1)} %copy-done, bf16[1024,1024]{1,0:T(8,128)(2,1)} %param.12, s32[]{:T(128)S(6)} %select_n.40), kind=kOutput, calls=%fused_computation.8 | convolution fusion | flops 1074266112 | bytes 4194308 | tf_op jit(solution)/shard_map/grad_sum/ti,tnc->nic/dot_general | solution.py:480
  19.4 1.6 collective-permute-start.3
  21.0 2.5 %fusion.5 = f32[4,512,256]{2,1,0:T(8,128)S(1)} fusion(bf16[1024,4,256]{2,1,0:T(4,128)(2,1)S(1)} %copy-done, bf16[1024,1024]{1,0:T(8,128)(2,1)} %param.12, s32[]{:T(128)S(6)} %select_n.39), kind=kOutput, calls=%fused_computation.6 | convolution fusion | flops 1073741824 | bytes 5242884 | tf_op jit(solution)/shard_map/grad_sum/ti,tnc->nic/dot_general | solution.py:480
  23.6 2.6 %fusion.trigger = bf16[4,528,256]{2,1,0:T(8,128)(2,1)} fusion(f32[4,16,256]{2,1,0:T(8,128)S(1)} %pad.12, f32[4,512,256]{2,1,0:T(8,128)S(1)} %fusion.5, bf16[4,528,256]{2,1,0:T(8,128)(2,1)} %collective-permute-done.3), kind=kLoop, calls=%fused_computation.1 | loop fusion | flops 2162688 | bytes 4325376 | tf_op jit(solution)/shard_map/grad_sum/convert_element_type | solution.py:486
  26.2 1.6 spread.1
  27.8 1.3 collective-permute-start.13
  29.1 2.6 %collective-permute-start.14 = (bf16[8,16,256]{2,1,0:T(8,128)(2,1)}, bf16[8,16,256]{2,1,0:T(8,128)(2,1)S(1)}, u32[]{:S(2)}, u32[]{:S(2)}) collective-permute-start(bf16[8,16,256]{2,1,0:T(8,128)(2,1)} %get-tuple-element.75.refs_0_), channel_id=1, source_target_pairs={{0,2},{1,3},{2,0},{3,1},{4,6},{5,7},{6,4},{7,5},{8,10},{9,11},{10,... | collective-permute-start | bytes 196616 | tf_op jit(solution)/shard_map/grad_sum/ppermute | solution.py:33
  31.7 1.1 collective-permute-start.15
  32.8 2.2 %collective-permute-done.14.refs_2_ = bf16[8,16,256]{2,1,0:T(8,128)(2,1)S(1)} collective-permute-done((bf16[8,16,256]{2,1,0:T(8,128)(2,1)}, bf16[8,16,256]{2,1,0:T(8,128)(2,1)S(1)}, u32[]{:S(2)}, u32[]{:S(2)}) %collective-permute-start.14) | collective-permute-done | bytes 65568 | tf_op jit(solution)/shard_map/grad_sum/ppermute | solution.py:33
  36.0 1.7 join.3
  37.8 0.8 dynamic-slice_bitcast_fusion
  38.5 0.9 collective-permute-start.4
  39.7 2.4 %collective-permute-start.6 = (bf16[528,256]{1,0:T(8,128)(2,1)S(1)}, bf16[528,256]{1,0:T(8,128)(2,1)S(1)}, u32[]{:S(2)}, u32[]{:S(2)}) collective-permute-start(bf16[528,256]{1,0:T(8,128)(2,1)S(1)} %get-tuple-element.117), channel_id=1, source_target_pairs={{0,192},{64,0},{128,64},{192,128},{1,193},{65,1},{129,65},{193,129... | collective-permute-start | bytes 811016 | tf_op jit(solution)/shard_map/grad_sum/ppermute | solution.py:493
  42.1 4.2 %collective-permute-done.4.a1 = bf16[528,256]{1,0:T(8,128)(2,1)S(1)} collective-permute-done((bf16[528,256]{1,0:T(8,128)(2,1)S(1)}, bf16[528,256]{1,0:T(8,128)(2,1)S(1)}, u32[]{:S(2)}, u32[]{:S(2)}) %collective-permute-start.4) | collective-permute-done | bytes 270368 | tf_op jit(solution)/shard_map/grad_sum/ppermute | solution.py:493
  46.3 7.9 %collective-permute-done.5.a2 = bf16[528,256]{1,0:T(8,128)(2,1)S(1)} collective-permute-done((bf16[528,256]{1,0:T(8,128)(2,1)S(1)}, bf16[528,256]{1,0:T(8,128)(2,1)S(1)}, u32[]{:S(2)}, u32[]{:S(2)}) %collective-permute-start.5) | collective-permute-done | bytes 270368 | tf_op jit(solution)/shard_map/grad_sum/ppermute | solution.py:493
  54.2 0.7 copy-done.21
  55.0 2.1 %sum_x.1.trigger = bf16[8,80,256]{2,1,0:T(8,128)(2,1)} custom-call(bf16[528,256]{1,0:T(8,128)(2,1)} %get-tuple-element.120.a0, bf16[528,256]{1,0:T(8,128)(2,1)} %copy-done.20, bf16[528,256]{1,0:T(8,128)(2,1)} %copy-done.21, bf16[528,256]{1,0:T(8,128)(2,1)} %copy-done.22), custom_call_target="tpu_custom_call" | custom-call | flops 1000000 | bytes 300000000 | tf_op jit(solution)/shard_map/grad_sum/sum_x/pallas_call | solution.py:497
  57.1 8.3 %all-to-all-start = ((bf16[8,80,256]{2,1,0:T(8,128)(2,1)}), bf16[8,80,256]{2,1,0:T(8,128)(2,1)S(1)}, u32[]{:S(2)}, u32[]{:S(2)}) async-start(bf16[8,80,256]{2,1,0:T(8,128)(2,1)} %sum_x.1.trigger), calls=%async_computation | async-start | bytes 655360 | tf_op jit(solution)/shard_map/grad_sum/all_to_all | solution.py:29
  65.4 0.8 collective-permute-start.7
  66.2 0.9 collective-permute-done.7.other
  67.7 1.4 choose.1
  69.1 2.7 %collective-permute-start.9 = (bf16[4,16,256]{2,1,0:T(8,128)(2,1)}, bf16[4,16,256]{2,1,0:T(8,128)(2,1)S(1)}, u32[]{:S(2)}, u32[]{:S(2)}) collective-permute-start(bf16[4,16,256]{2,1,0:T(8,128)(2,1)} %get-tuple-element.73), channel_id=1, source_target_pairs={{0,3},{1,0},{2,1},{3,2},{4,7},{5,4},{6,5},{7,6},{8,11},{9,8},{10,9... | collective-permute-start | bytes 98312 | tf_op jit(solution)/shard_map/grad_sum/ppermute | solution.py:33
  72.5 1.2 collective-permute-done.8.refs_1_
  73.7 2.9 %collective-permute-done.10.refs_3_ = bf16[4,16,256]{2,1,0:T(8,128)(2,1)S(1)} collective-permute-done((bf16[4,16,256]{2,1,0:T(8,128)(2,1)}, bf16[4,16,256]{2,1,0:T(8,128)(2,1)S(1)}, u32[]{:S(2)}, u32[]{:S(2)}) %collective-permute-start.10) | collective-permute-done | bytes 32800 | tf_op jit(solution)/shard_map/grad_sum/ppermute | solution.py:33
  77.2 1.5 join.2
  78.7 2.9 %all-to-all-done = bf16[8,80,256]{2,1,0:T(8,128)(2,1)S(1)} async-done(((bf16[8,80,256]{2,1,0:T(8,128)(2,1)}), bf16[8,80,256]{2,1,0:T(8,128)(2,1)S(1)}, u32[]{:S(2)}, u32[]{:S(2)}) %all-to-all-start) | async-done | bytes 327712 | tf_op jit(solution)/shard_map/grad_sum/all_to_all | solution.py:29
  82.4 0.7 broadcast_in_dim.39
  83.1 3.8 %all-to-all-start.1 = ((bf16[8,80,256]{2,1,0:T(8,128)(2,1)}), bf16[8,80,256]{2,1,0:T(8,128)(2,1)S(1)}, u32[]{:S(2)}, u32[]{:S(2)}) async-start(bf16[8,80,256]{2,1,0:T(8,128)(2,1)} %broadcast_in_dim.39), calls=%async_computation.1 | async-start | bytes 655360 | tf_op jit(solution)/shard_map/grad_all/all_to_all | solution.py:29
  86.9 10.4 %all-to-all-done.1 = bf16[8,80,256]{2,1,0:T(8,128)(2,1)S(1)} async-done(((bf16[8,80,256]{2,1,0:T(8,128)(2,1)}), bf16[8,80,256]{2,1,0:T(8,128)(2,1)S(1)}, u32[]{:S(2)}, u32[]{:S(2)}) %all-to-all-start.1) | async-done | bytes 327712 | tf_op jit(solution)/shard_map/grad_all/all_to_all | solution.py:29
  97.5 3.9 %collective-permute-start.16 = (bf16[8,40,16,256]{3,2,1,0:T(8,128)(2,1)}, bf16[8,40,16,256]{3,2,1,0:T(8,128)(2,1)}, u32[]{:S(2)}, u32[]{:S(2)}) collective-permute-start(bf16[8,40,16,256]{3,2,1,0:T(8,128)(2,1)} %bitcast.41), channel_id=1, source_target_pairs={{0,4},{4,0},{1,5},{5,1},{2,6},{6,2},{3,7},{7,3},{8,12},{12,8},{9,1... | collective-permute-start | bytes 7864328 | tf_op jit(solution)/shard_map/grad_all/ppermute | solution.py:25
  101.6 2.5 %collective-permute-start.17 = (bf16[512,256]{1,0:T(8,128)(2,1)S(1)}, bf16[512,256]{1,0:T(8,128)(2,1)S(1)}, u32[]{:S(2)}, u32[]{:S(2)}) collective-permute-start(bf16[512,256]{1,0:T(8,128)(2,1)S(1)} %bitcast.45), channel_id=1, source_target_pairs={{0,3},{1,0},{2,1},{3,2},{4,7},{5,4},{6,5},{7,6},{8,11},{9,8},{10,9... | collective-permute-start | bytes 786440 | tf_op jit(solution)/shard_map/grad_all/ppermute | solution.py:33
  108.5 1.4 stack.51.where
  110.7 0.7 collective-permute-start.19
  111.4 3.6 %collective-permute-done.17.refs_3_ = bf16[512,256]{1,0:T(8,128)(2,1)S(1)} collective-permute-done((bf16[512,256]{1,0:T(8,128)(2,1)S(1)}, bf16[512,256]{1,0:T(8,128)(2,1)S(1)}, u32[]{:S(2)}, u32[]{:S(2)}) %collective-permute-start.17) | collective-permute-done | bytes 262176 | tf_op jit(solution)/shard_map/grad_all/ppermute | solution.py:33
  115.0 1.3 collective-permute-start.21
  116.3 1.8 copy-done.1
  118.1 2.6 %prep.1 = (bf16[1024,1024]{1,0:T(8,128)(2,1)S(1)}, bf16[1024,1024]{1,0:T(8,128)(2,1)S(1)}) custom-call(s32[9]{0:T(128)S(1)} %stack.51.where, bf16[8,40,16,256]{3,2,1,0:T(8,128)(2,1)S(1)} %bitcast.42, bf16[8,40,16,256]{3,2,1,0:T(8,128)(2,1)} %collective-permute-done.16.oth), custom_call_target="tpu_custom_call" | custom-call | tf_op jit(solution)/shard_map/grad_all/prep/pallas_call | solution.py:74
  120.9 1.5 collective-permute-done.20.refs_6_
  122.4 5.9 %rotate.1 = (bf16[1024,1024]{1,0:T(8,128)(2,1)S(1)}, bf16[1024,1024]{1,0:T(8,128)(2,1)S(1)}, bf16[4,512,256]{2,1,0:T(8,128)(2,1)S(1)}, bf16[4,16,256]{2,1,0:T(8,128)(2,1)S(1)}) custom-call(s32[9]{0:T(128)S(1)} %stack.51.where, bf16[512,256]{1,0:T(8,128)(2,1)S(1)} %bitcast.48, bf16[512,256]{1,0:T(8,128)(2,1)S(1)} %collective-permute-done.11.refs_1_, ...), custom_call_target="tpu_custom_call" | custom-call | tf_op jit(solution)/shard_map/rotate/rotate/pallas_call | solution.py:545
  128.3 0.9 copy-done.9
  129.2 1.3 copy-done.14
  130.5 1.4 copy-done.16
  131.9 4.6 %all-to-all-start.2 = ((bf16[4,512,256]{2,1,0:T(8,128)(2,1)}), bf16[4,512,256]{2,1,0:T(8,128)(2,1)S(1)}, u32[]{:S(2)}, u32[]{:S(2)}) async-start(bf16[4,512,256]{2,1,0:T(8,128)(2,1)} %copy-done.9), calls=%async_computation.2 | async-start | bytes 2097152 | tf_op jit(solution)/shard_map/rotate/all_to_all | solution.py:29
  136.6 1.6 copy-done.4
  138.2 1.6 copy-done.7
  139.8 1.3 copy-done.18
  141.1 3.0 %old_power.1.old = f32[1024,1024]{1,0:T(8,128)S(1)} custom-call(s32[9]{0:T(128)S(1)} %stack.51.where, bf16[8,20,16,256]{3,2,1,0:T(8,128)(2,1)S(1)} %bitcast.49, bf16[1024,1024]{1,0:T(8,128)(2,1)S(1)} %copy-done.4, bf16[1024,1024]{1,0:T(8,128)(2,1)S(1)} %copy-done.7), custom_call_target="tpu_custom_call" | custom-call | flops 6000000000 | bytes 24000000 | tf_op jit(solution)/shard_map/power/old_power/pallas_call | solution.py:74
  144.1 6.9 %power.1 = (bf16[4,32,256]{2,1,0:T(8,128)(2,1)S(1)}, bf16[4,32,256]{2,1,0:T(8,128)(2,1)S(1)}) custom-call(s32[9]{0:T(128)S(1)} %stack.51.where, bf16[1024,1024]{1,0:T(8,128)(2,1)S(1)} %copy-done.15, bf16[1024,1024]{1,0:T(8,128)(2,1)S(1)} %copy-done.17, f32[1024,1024]{1,0:T(8,128)S(1)} %old_power.1.old), custom_call_target="tpu_custom_call" | custom-call | flops 6000000000 | bytes 24000000 | tf_op jit(solution)/shard_map/power/power/pallas_call | solution.py:74
  151.0 0.8 all-to-all-done.2.direct
  151.8 1.7 copy-done.8
  153.5 1.0 back.1.own
  155.1 1.2 collective-permute-done.22.oth
  156.3 1.2 update.1
  158.0 1.2 collective-permute-start.24
  159.2 1.3 collective-permute-start.25
  160.5 13.5 %collective-permute-done.23.g1 = bf16[608,256]{1,0:T(8,128)(2,1)S(1)} collective-permute-done((bf16[608,256]{1,0:T(8,128)(2,1)S(1)}, bf16[608,256]{1,0:T(8,128)(2,1)S(1)}, u32[]{:S(2)}, u32[]{:S(2)}) %collective-permute-start.23) | collective-permute-done | bytes 311328 | tf_op jit(solution)/shard_map/home/ppermute | solution.py:37
  175.0 1.6 collective-permute-start.26
  176.6 1.3 collective-permute-done.26.recv
  177.9 1.5 final.1
  (119 shorter events, 11.1 us)
Async XLA Ops:
  7.2 9.6 %copy-start = (bf16[1024,4,256]{2,1,0:T(4,128)(2,1)S(1)}, bf16[1024,4,256]{2,1,0:T(4,128)(2,1)}, u32[]{:S(2)}) copy-start(bf16[1024,4,256]{2,1,0:T(4,128)(2,1)} %param.13) | copy-start | bytes 6291460
  7.2 90.3 %all-gather.5.cloned.1.call-start = ((), (), s32[]{:S(2)}) async-start(), calls=%async_computation.3 | async-start | bytes 2949120 | tf_op jit(solution)/shard_map/grad_sum/all_gather | solution.py:490
  9.1 10.2 %collective-permute-start = (bf16[6,16,256]{2,1,0:T(8,128)(2,1)}, bf16[6,16,256]{2,1,0:T(8,128)(2,1)S(1)}, u32[]{:S(2)}, u32[]{:S(2)}) collective-permute-start(bf16[6,16,256]{2,1,0:T(8,128)(2,1)} %get-tuple-element.61), channel_id=1, source_target_pairs={{0,64},{64,128},{128,192},{192,0},{1,65},{65,129},{129,193},{193,1... | collective-permute-start | bytes 147464 | tf_op jit(solution)/shard_map/state_rows/ppermute | solution.py:472
  11.2 8.1 %collective-permute-start.1 = (bf16[6,16,256]{2,1,0:T(8,128)(2,1)}, bf16[6,16,256]{2,1,0:T(8,128)(2,1)S(1)}, u32[]{:S(2)}, u32[]{:S(2)}) collective-permute-start(bf16[6,16,256]{2,1,0:T(8,128)(2,1)} %get-tuple-element.62), channel_id=1, source_target_pairs={{0,128},{64,192},{128,0},{192,64},{1,129},{65,193},{129,1},{193,65... | collective-permute-start | bytes 147464 | tf_op jit(solution)/shard_map/state_rows/ppermute | solution.py:472
  13.7 5.7 %collective-permute-start.2 = (bf16[6,16,256]{2,1,0:T(8,128)(2,1)}, bf16[6,16,256]{2,1,0:T(8,128)(2,1)S(1)}, u32[]{:S(2)}, u32[]{:S(2)}) collective-permute-start(bf16[6,16,256]{2,1,0:T(8,128)(2,1)} %get-tuple-element.63), channel_id=1, source_target_pairs={{0,192},{64,0},{128,64},{192,128},{1,193},{65,1},{129,65},{193,129... | collective-permute-start | bytes 147464 | tf_op jit(solution)/shard_map/state_rows/ppermute | solution.py:472
  19.4 4.2 %copy-start.26 = (bf16[6,16,256]{2,1,0:T(8,128)(2,1)}, bf16[6,16,256]{2,1,0:T(8,128)(2,1)S(1)}, u32[]{:S(2)}) copy-start(bf16[6,16,256]{2,1,0:T(8,128)(2,1)S(1)} %collective-permute-done.r1) | copy-start | bytes 147460
  19.4 4.2 %copy-start.27 = (bf16[6,16,256]{2,1,0:T(8,128)(2,1)}, bf16[6,16,256]{2,1,0:T(8,128)(2,1)S(1)}, u32[]{:S(2)}) copy-start(bf16[6,16,256]{2,1,0:T(8,128)(2,1)S(1)} %collective-permute-done.1.r2) | copy-start | bytes 147460
  19.4 4.1 %copy-start.28 = (bf16[6,16,256]{2,1,0:T(8,128)(2,1)}, bf16[6,16,256]{2,1,0:T(8,128)(2,1)S(1)}, u32[]{:S(2)}) copy-start(bf16[6,16,256]{2,1,0:T(8,128)(2,1)S(1)} %collective-permute-done.2.r3) | copy-start | bytes 147460
  19.4 4.1 %collective-permute-start.3 = (bf16[4,528,256]{2,1,0:T(8,128)(2,1)S(1)}, bf16[4,528,256]{2,1,0:T(8,128)(2,1)}, u32[]{:S(2)}, u32[]{:S(2)}) collective-permute-start(bf16[4,528,256]{2,1,0:T(8,128)(2,1)S(1)} %pad_maximum_fusion), channel_id=1, source_target_pairs={{0,4},{4,0},{1,5},{5,1},{2,6},{6,2},{3,7},{7,3},{8,12},{12,8},{9,1... | collective-permute-start | bytes 3244040 | tf_op jit(solution)/shard_map/grad_sum/ppermute | solution.py:25
  26.1 11.6 %copy-start.19 = (bf16[4,528,256]{2,1,0:T(8,128)(2,1)S(1)}, bf16[4,528,256]{2,1,0:T(8,128)(2,1)}, u32[]{:S(2)}) copy-start(bf16[4,528,256]{2,1,0:T(8,128)(2,1)} %fusion.trigger) | copy-start | bytes 3244036
  27.8 5.0 %collective-permute-start.13 = (bf16[8,16,256]{2,1,0:T(8,128)(2,1)}, bf16[8,16,256]{2,1,0:T(8,128)(2,1)S(1)}, u32[]{:S(2)}, u32[]{:S(2)}) collective-permute-start(bf16[8,16,256]{2,1,0:T(8,128)(2,1)} %get-tuple-element.75.refs_0_), channel_id=1, source_target_pairs={{0,1},{1,2},{2,3},{3,0},{4,5},{5,6},{6,7},{7,4},{8,9},{9,10},{10,1... | collective-permute-start | bytes 196616 | tf_op jit(solution)/shard_map/grad_sum/ppermute | solution.py:33
  29.1 5.9 %collective-permute-start.14 = (bf16[8,16,256]{2,1,0:T(8,128)(2,1)}, bf16[8,16,256]{2,1,0:T(8,128)(2,1)S(1)}, u32[]{:S(2)}, u32[]{:S(2)}) collective-permute-start(bf16[8,16,256]{2,1,0:T(8,128)(2,1)} %get-tuple-element.75.refs_0_), channel_id=1, source_target_pairs={{0,2},{1,3},{2,0},{3,1},{4,6},{5,7},{6,4},{7,5},{8,10},{9,11},{10,... | collective-permute-start | bytes 196616 | tf_op jit(solution)/shard_map/grad_sum/ppermute | solution.py:33
  31.7 3.6 %collective-permute-start.15 = (bf16[8,16,256]{2,1,0:T(8,128)(2,1)}, bf16[8,16,256]{2,1,0:T(8,128)(2,1)S(1)}, u32[]{:S(2)}, u32[]{:S(2)}) collective-permute-start(bf16[8,16,256]{2,1,0:T(8,128)(2,1)} %get-tuple-element.75.refs_0_), channel_id=1, source_target_pairs={{0,3},{1,0},{2,1},{3,2},{4,7},{5,4},{6,5},{7,6},{8,11},{9,8},{10,9... | collective-permute-start | bytes 196616 | tf_op jit(solution)/shard_map/grad_sum/ppermute | solution.py:33
  32.8 2.6 %copy-start.23 = (bf16[8,16,256]{2,1,0:T(8,128)(2,1)}, bf16[8,16,256]{2,1,0:T(8,128)(2,1)S(1)}, u32[]{:S(2)}) copy-start(bf16[8,16,256]{2,1,0:T(8,128)(2,1)S(1)} %collective-permute-done.13.refs_1_) | copy-start | bytes 196612
  37.7 27.6 %copy-start.36 = (bf16[4,16,256]{2,1,0:T(8,128)(2,1)S(1)}, bf16[4,16,256]{2,1,0:T(8,128)(2,1)}, u32[]{:S(2)}) copy-start(bf16[4,16,256]{2,1,0:T(8,128)(2,1)} %get-tuple-element.70) | copy-start | bytes 98308
  38.5 43.2 %copy-start.34 = (f32[32]{0:T(128)S(1)}, f32[32]{0:T(128)}, u32[]{:S(2)}) copy-start(f32[32]{0:T(128)} %param.22) | copy-start | bytes 388
  38.5 43.2 %copy-start.35 = (f32[32]{0:T(128)S(1)}, f32[32]{0:T(128)}, u32[]{:S(2)}) copy-start(f32[32]{0:T(128)} %param.23) | copy-start | bytes 388
  38.5 7.8 %collective-permute-start.4 = (bf16[528,256]{1,0:T(8,128)(2,1)S(1)}, bf16[528,256]{1,0:T(8,128)(2,1)S(1)}, u32[]{:S(2)}, u32[]{:S(2)}) collective-permute-start(bf16[528,256]{1,0:T(8,128)(2,1)S(1)} %get-tuple-element.119), channel_id=1, source_target_pairs={{0,128},{64,192},{128,0},{192,64},{1,129},{65,193},{129,1},{193,65... | collective-permute-start | bytes 811016 | tf_op jit(solution)/shard_map/grad_sum/ppermute | solution.py:493
  39.4 14.8 %collective-permute-start.5 = (bf16[528,256]{1,0:T(8,128)(2,1)S(1)}, bf16[528,256]{1,0:T(8,128)(2,1)S(1)}, u32[]{:S(2)}, u32[]{:S(2)}) collective-permute-start(bf16[528,256]{1,0:T(8,128)(2,1)S(1)} %get-tuple-element.118), channel_id=1, source_target_pairs={{0,64},{64,128},{128,192},{192,0},{1,65},{65,129},{129,193},{193,1... | collective-permute-start | bytes 811016 | tf_op jit(solution)/shard_map/grad_sum/ppermute | solution.py:493
  39.7 14.6 %collective-permute-start.6 = (bf16[528,256]{1,0:T(8,128)(2,1)S(1)}, bf16[528,256]{1,0:T(8,128)(2,1)S(1)}, u32[]{:S(2)}, u32[]{:S(2)}) collective-permute-start(bf16[528,256]{1,0:T(8,128)(2,1)S(1)} %get-tuple-element.117), channel_id=1, source_target_pairs={{0,192},{64,0},{128,64},{192,128},{1,193},{65,1},{129,65},{193,129... | collective-permute-start | bytes 811016 | tf_op jit(solution)/shard_map/grad_sum/ppermute | solution.py:493
  46.3 7.9 %copy-start.20 = (bf16[528,256]{1,0:T(8,128)(2,1)}, bf16[528,256]{1,0:T(8,128)(2,1)S(1)}, u32[]{:S(2)}) copy-start(bf16[528,256]{1,0:T(8,128)(2,1)S(1)} %collective-permute-done.4.a1) | copy-start | bytes 811012
  54.2 0.8 copy-start.22
  57.1 47.5 %copy-start.33 = (s32[5]{0:T(128)S(1)}, s32[5]{0:T(128)}, u32[]{:S(2)}) copy-start(s32[5]{0:T(128)} %param.15) | copy-start | bytes 64
  57.1 24.5 %all-to-all-start = ((bf16[8,80,256]{2,1,0:T(8,128)(2,1)}), bf16[8,80,256]{2,1,0:T(8,128)(2,1)S(1)}, u32[]{:S(2)}, u32[]{:S(2)}) async-start(bf16[8,80,256]{2,1,0:T(8,128)(2,1)} %sum_x.1.trigger), calls=%async_computation | async-start | bytes 655360 | tf_op jit(solution)/shard_map/grad_sum/all_to_all | solution.py:29
  65.4 1.7 collective-permute-start.7
  69.1 4.6 %collective-permute-start.8 = (bf16[4,16,256]{2,1,0:T(8,128)(2,1)}, bf16[4,16,256]{2,1,0:T(8,128)(2,1)S(1)}, u32[]{:S(2)}, u32[]{:S(2)}) collective-permute-start(bf16[4,16,256]{2,1,0:T(8,128)(2,1)} %get-tuple-element.72), channel_id=1, source_target_pairs={{0,1},{1,2},{2,3},{3,0},{4,5},{5,6},{6,7},{7,4},{8,9},{9,10},{10,1... | collective-permute-start | bytes 98312 | tf_op jit(solution)/shard_map/grad_sum/ppermute | solution.py:33
  69.1 4.6 %collective-permute-start.9 = (bf16[4,16,256]{2,1,0:T(8,128)(2,1)}, bf16[4,16,256]{2,1,0:T(8,128)(2,1)S(1)}, u32[]{:S(2)}, u32[]{:S(2)}) collective-permute-start(bf16[4,16,256]{2,1,0:T(8,128)(2,1)} %get-tuple-element.73), channel_id=1, source_target_pairs={{0,3},{1,0},{2,1},{3,2},{4,7},{5,4},{6,5},{7,6},{8,11},{9,8},{10,9... | collective-permute-start | bytes 98312 | tf_op jit(solution)/shard_map/grad_sum/ppermute | solution.py:33
  71.8 4.8 %collective-permute-start.10 = (bf16[4,16,256]{2,1,0:T(8,128)(2,1)}, bf16[4,16,256]{2,1,0:T(8,128)(2,1)S(1)}, u32[]{:S(2)}, u32[]{:S(2)}) collective-permute-start(bf16[4,16,256]{2,1,0:T(8,128)(2,1)} %get-tuple-element.73), channel_id=1, source_target_pairs={{0,2},{1,3},{2,0},{3,1},{4,6},{5,7},{6,4},{7,5},{8,10},{9,11},{10,... | collective-permute-start | bytes 98312 | tf_op jit(solution)/shard_map/grad_sum/ppermute | solution.py:33
  73.7 2.9 %copy-start.29 = (bf16[4,16,256]{2,1,0:T(8,128)(2,1)}, bf16[4,16,256]{2,1,0:T(8,128)(2,1)S(1)}, u32[]{:S(2)}) copy-start(bf16[4,16,256]{2,1,0:T(8,128)(2,1)S(1)} %collective-permute-done.8.refs_1_) | copy-start | bytes 98308
  73.7 2.9 %copy-start.30 = (bf16[4,16,256]{2,1,0:T(8,128)(2,1)}, bf16[4,16,256]{2,1,0:T(8,128)(2,1)S(1)}, u32[]{:S(2)}) copy-start(bf16[4,16,256]{2,1,0:T(8,128)(2,1)S(1)} %collective-permute-done.9.refs_2_) | copy-start | bytes 98308
  83.1 14.2 %all-to-all-start.1 = ((bf16[8,80,256]{2,1,0:T(8,128)(2,1)}), bf16[8,80,256]{2,1,0:T(8,128)(2,1)S(1)}, u32[]{:S(2)}, u32[]{:S(2)}) async-start(bf16[8,80,256]{2,1,0:T(8,128)(2,1)} %broadcast_in_dim.39), calls=%async_computation.1 | async-start | bytes 655360 | tf_op jit(solution)/shard_map/grad_all/all_to_all | solution.py:29
  86.9 49.7 %all-gather.7.cloned.1.call-start = ((), (), s32[]{:S(2)}) async-start(), calls=%async_computation.4 | async-start | bytes 1474560 | tf_op jit(solution)/shard_map/grad_sum/all_gather | solution.py:511
  97.5 18.8 %collective-permute-start.16 = (bf16[8,40,16,256]{3,2,1,0:T(8,128)(2,1)}, bf16[8,40,16,256]{3,2,1,0:T(8,128)(2,1)}, u32[]{:S(2)}, u32[]{:S(2)}) collective-permute-start(bf16[8,40,16,256]{3,2,1,0:T(8,128)(2,1)} %bitcast.41), channel_id=1, source_target_pairs={{0,4},{4,0},{1,5},{5,1},{2,6},{6,2},{3,7},{7,3},{8,12},{12,8},{9,1... | collective-permute-start | bytes 7864328 | tf_op jit(solution)/shard_map/grad_all/ppermute | solution.py:25
  101.4 9.3 %collective-permute-start.11 = (bf16[512,256]{1,0:T(8,128)(2,1)S(1)}, bf16[512,256]{1,0:T(8,128)(2,1)S(1)}, u32[]{:S(2)}, u32[]{:S(2)}) collective-permute-start(bf16[512,256]{1,0:T(8,128)(2,1)S(1)} %bitcast.44), channel_id=1, source_target_pairs={{0,1},{1,2},{2,3},{3,0},{4,5},{5,6},{6,7},{7,4},{8,9},{9,10},{10,1... | collective-permute-start | bytes 786440 | tf_op jit(solution)/shard_map/grad_all/ppermute | solution.py:33
  101.6 13.4 %collective-permute-start.17 = (bf16[512,256]{1,0:T(8,128)(2,1)S(1)}, bf16[512,256]{1,0:T(8,128)(2,1)S(1)}, u32[]{:S(2)}, u32[]{:S(2)}) collective-permute-start(bf16[512,256]{1,0:T(8,128)(2,1)S(1)} %bitcast.45), channel_id=1, source_target_pairs={{0,3},{1,0},{2,1},{3,2},{4,7},{5,4},{6,5},{7,6},{8,11},{9,8},{10,9... | collective-permute-start | bytes 786440 | tf_op jit(solution)/shard_map/grad_all/ppermute | solution.py:33
  104.2 16.6 %collective-permute-start.12 = (bf16[512,256]{1,0:T(8,128)(2,1)S(1)}, bf16[512,256]{1,0:T(8,128)(2,1)S(1)}, u32[]{:S(2)}, u32[]{:S(2)}) collective-permute-start(bf16[512,256]{1,0:T(8,128)(2,1)S(1)} %bitcast.46), channel_id=1, source_target_pairs={{0,2},{1,3},{2,0},{3,1},{4,6},{5,7},{6,4},{7,5},{8,10},{9,11},{10,... | collective-permute-start | bytes 786440 | tf_op jit(solution)/shard_map/grad_all/ppermute | solution.py:33
  109.8 11.0 %collective-permute-start.18 = (bf16[512,256]{1,0:T(8,128)(2,1)S(1)}, bf16[512,256]{1,0:T(8,128)(2,1)S(1)}, u32[]{:S(2)}, u32[]{:S(2)}) collective-permute-start(bf16[512,256]{1,0:T(8,128)(2,1)S(1)} %bitcast.47), channel_id=1, source_target_pairs={{0,4},{4,0},{1,5},{5,1},{2,6},{6,2},{3,7},{7,3},{8,12},{12,8},{9,1... | collective-permute-start | bytes 786440 | tf_op jit(solution)/shard_map/grad_all/ppermute | solution.py:25
  110.7 10.1 %collective-permute-start.19 = (bf16[512,256]{1,0:T(8,128)(2,1)S(1)}, bf16[512,256]{1,0:T(8,128)(2,1)S(1)}, u32[]{:S(2)}, u32[]{:S(2)}) collective-permute-start(bf16[512,256]{1,0:T(8,128)(2,1)S(1)} %collective-permute-done.11.refs_1_), channel_id=1, source_target_pairs={{0,4},{4,0},{1,5},{5,1},{2,6},{6,2},{3,7},{7,3},{8,12},{12,8},{9,1... | collective-permute-start | bytes 786440 | tf_op jit(solution)/shard_map/grad_all/ppermute | solution.py:25
  115.0 5.8 %collective-permute-start.21 = (bf16[512,256]{1,0:T(8,128)(2,1)S(1)}, bf16[512,256]{1,0:T(8,128)(2,1)S(1)}, u32[]{:S(2)}, u32[]{:S(2)}) collective-permute-start(bf16[512,256]{1,0:T(8,128)(2,1)S(1)} %collective-permute-done.17.refs_3_), channel_id=1, source_target_pairs={{0,4},{4,0},{1,5},{5,1},{2,6},{6,2},{3,7},{7,3},{8,12},{12,8},{9,1... | collective-permute-start | bytes 786440 | tf_op jit(solution)/shard_map/grad_all/ppermute | solution.py:25
  116.3 1.8 copy-start.1
  118.1 4.3 %copy-start.2 = (bf16[320,16,256]{2,1,0:T(8,128)(2,1)S(1)}, bf16[320,16,256]{2,1,0:T(8,128)(2,1)}, u32[]{:S(2)}) copy-start(bf16[320,16,256]{2,1,0:T(8,128)(2,1)} %all-gather.5.cloned.1.call-done) | copy-start | bytes 7864324
  120.7 7.5 %copy-start.3 = (bf16[1024,1024]{1,0:T(8,128)(2,1)}, bf16[1024,1024]{1,0:T(8,128)(2,1)S(1)}, u32[]{:S(2)}) copy-start(bf16[1024,1024]{1,0:T(8,128)(2,1)S(1)} %get-tuple-element.81.refs_8_.left) | copy-start | bytes 6291460
  120.7 7.5 %copy-start.6 = (bf16[1024,1024]{1,0:T(8,128)(2,1)}, bf16[1024,1024]{1,0:T(8,128)(2,1)S(1)}, u32[]{:S(2)}) copy-start(bf16[1024,1024]{1,0:T(8,128)(2,1)S(1)} %get-tuple-element.82.refs_9_.right) | copy-start | bytes 6291460
  120.7 1.6 collective-permute-start.20
  128.3 1.0 copy-start.9
  129.2 1.3 copy-start.14
  130.5 1.4 copy-start.16
  131.9 19.9 %all-to-all-start.2 = ((bf16[4,512,256]{2,1,0:T(8,128)(2,1)}), bf16[4,512,256]{2,1,0:T(8,128)(2,1)S(1)}, u32[]{:S(2)}, u32[]{:S(2)}) async-start(bf16[4,512,256]{2,1,0:T(8,128)(2,1)} %copy-done.9), calls=%async_computation.2 | async-start | bytes 2097152 | tf_op jit(solution)/shard_map/rotate/all_to_all | solution.py:29
  136.6 1.6 copy-start.4
  138.2 1.6 copy-start.7
  139.8 1.3 copy-start.18
  141.1 3.0 %copy-start.15 = (bf16[1024,1024]{1,0:T(8,128)(2,1)S(1)}, bf16[1024,1024]{1,0:T(8,128)(2,1)}, u32[]{:S(2)}) copy-start(bf16[1024,1024]{1,0:T(8,128)(2,1)} %copy-done.14) | copy-start | bytes 6291460
  141.1 3.0 %copy-start.17 = (bf16[1024,1024]{1,0:T(8,128)(2,1)S(1)}, bf16[1024,1024]{1,0:T(8,128)(2,1)}, u32[]{:S(2)}) copy-start(bf16[1024,1024]{1,0:T(8,128)(2,1)} %copy-done.16) | copy-start | bytes 6291460
  151.8 4.5 %copy-start.5 = (bf16[1024,1024]{1,0:T(8,128)(2,1)S(1)}, bf16[1024,1024]{1,0:T(8,128)(2,1)}, u32[]{:S(2)}) copy-start(bf16[1024,1024]{1,0:T(8,128)(2,1)} %copy-done.3) | copy-start | bytes 6291460
  151.8 1.7 copy-start.8
  154.6 23.3 %copy-start.10 = (f32[4,16,256]{2,1,0:T(8,128)S(1)}, f32[4,16,256]{2,1,0:T(8,128)}, u32[]{:S(2)}) copy-start(f32[4,16,256]{2,1,0:T(8,128)} %m1.1) | copy-start | bytes 196612
  154.6 23.3 %copy-start.11 = (f32[4,16,256]{2,1,0:T(8,128)S(1)}, f32[4,16,256]{2,1,0:T(8,128)}, u32[]{:S(2)}) copy-start(f32[4,16,256]{2,1,0:T(8,128)} %m2.1) | copy-start | bytes 196612
  154.6 23.3 %copy-start.12 = (f32[4,16,256]{2,1,0:T(8,128)S(1)}, f32[4,16,256]{2,1,0:T(8,128)}, u32[]{:S(2)}) copy-start(f32[4,16,256]{2,1,0:T(8,128)} %sl.1) | copy-start | bytes 196612
  154.6 23.3 %copy-start.13 = (f32[4,16,256]{2,1,0:T(8,128)S(1)}, f32[4,16,256]{2,1,0:T(8,128)}, u32[]{:S(2)}) copy-start(f32[4,16,256]{2,1,0:T(8,128)} %sr.1) | copy-start | bytes 196612
  154.6 1.6 collective-permute-start.22
  157.5 16.5 %collective-permute-start.23 = (bf16[608,256]{1,0:T(8,128)(2,1)S(1)}, bf16[608,256]{1,0:T(8,128)(2,1)S(1)}, u32[]{:S(2)}, u32[]{:S(2)}) collective-permute-start(bf16[608,256]{1,0:T(8,128)(2,1)S(1)} %get-tuple-element.97), channel_id=1, source_target_pairs={{0,64},{64,128},{128,192},{192,0},{1,65},{65,129},{129,193},{193,1... | collective-permute-start | bytes 933896 | tf_op jit(solution)/shard_map/home/ppermute | solution.py:37
  158.0 16.1 %collective-permute-start.24 = (bf16[608,256]{1,0:T(8,128)(2,1)S(1)}, bf16[608,256]{1,0:T(8,128)(2,1)S(1)}, u32[]{:S(2)}, u32[]{:S(2)}) collective-permute-start(bf16[608,256]{1,0:T(8,128)(2,1)S(1)} %get-tuple-element.98), channel_id=1, source_target_pairs={{0,128},{64,192},{128,0},{192,64},{1,129},{65,193},{129,1},{193,65... | collective-permute-start | bytes 933896 | tf_op jit(solution)/shard_map/home/ppermute | solution.py:37
  159.2 15.2 %collective-permute-start.25 = (bf16[608,256]{1,0:T(8,128)(2,1)S(1)}, bf16[608,256]{1,0:T(8,128)(2,1)S(1)}, u32[]{:S(2)}, u32[]{:S(2)}) collective-permute-start(bf16[608,256]{1,0:T(8,128)(2,1)S(1)} %get-tuple-element.99), channel_id=1, source_target_pairs={{0,192},{64,0},{128,64},{192,128},{1,193},{65,1},{129,65},{193,129... | collective-permute-start | bytes 933896 | tf_op jit(solution)/shard_map/home/ppermute | solution.py:37
  175.0 2.9 %collective-permute-start.26 = (bf16[704,256]{1,0:T(8,128)(2,1)S(1)}, bf16[704,256]{1,0:T(8,128)(2,1)S(1)}, u32[]{:S(2)}, u32[]{:S(2)}) collective-permute-start(bf16[704,256]{1,0:T(8,128)(2,1)S(1)} %get-tuple-element.101), channel_id=1, source_target_pairs={{0,4},{4,0},{1,5},{5,1},{2,6},{6,2},{3,7},{7,3},{8,12},{12,8},{9,1... | collective-permute-start | bytes 1081352 | tf_op jit(solution)/shard_map/home/ppermute | solution.py:25
  (5 other events, 3.2 us)
Sparse Core Ops, SparseCore 0:
  37.8 48.2 all-gather.4
  101.5 28.1 all-gather.6
